TPU v7x, 128 devices: a whole 4x4x4 slice. The times are simulated.
128 devices in a mesh: ta: 16 (over z, x_hi, core), ha: 2 (over x_lo), wa: 4 (over y).
Axes of the slice: x: 4 (x_hi: 2, x_lo: 2; x = x_hi * 2 + x_lo), y: 4, z: 4, core: 2. Of those that a mesh axis runs over, the one named last changes fastest.
Arguments:
- video_in: float32 [64, 16, 64, 128], P('ta', 'ha', 'wa'), may hold values from -6 to 6
- first_filter: float32 [27, 128, 128], replicated, may hold values from -0.109375 to 0.109375
- first_bias: float32 [128], replicated, may hold values from -3 to 3
- second_filter: float32 [27, 128, 128], replicated, may hold values from -0.109375 to 0.109375
- grad_output: float32 [64, 16, 64, 128], P('ta', 'ha', 'wa'), may hold values from -8 to 8
Outputs:
- grad_input: float32 [64, 16, 64, 128], P('ta', 'ha', 'wa')
- grad_first: float32 [3456, 128], P('ta')
- grad_second: float32 [3456, 128], P('ta')
- grad_bias: float32 [128], replicated
All inputs are finite; a program needn't handle non-finite values.
Results may differ from a plain program's by a relative error of at most 0.00018.
Values sent between devices are 32-bit elements; how exact they have to be, the bound alone decides.
A program may use at most 128 MiB of HBM per device.

v0:
```python
import jax
import jax.numpy as jnp
from jax import lax
from jax.sharding import PartitionSpec as P

HIGHEST = lax.Precision.HIGHEST


def passed_along(array, axis, by):
    length = lax.axis_size(axis)
    pairs = [(i, i + by) for i in range(length) if 0 <= i + by < length]
    return lax.ppermute(array, axis, pairs)


def extended_2(block, sides, width):
    for axis, dim in sides:
        count = lax.axis_size(axis)
        forward = [(i, i + 1) for i in range(count - 1)]
        backward = [(target, source) for source, target in forward]
        low = lax.ppermute(
            lax.slice_in_dim(block, block.shape[dim] - width, None, axis=dim), axis, forward
        )
        high = lax.ppermute(lax.slice_in_dim(block, 0, width, axis=dim), axis, backward)
        block = jnp.concatenate([low, block, high], axis=dim)
    return block


def plane_columns(extended, start_t, flipped, frames, height, breadth):
    pieces = []
    for tap_h in range(3):
        for tap_w in range(3):
            off_h = 2 - tap_h if flipped else tap_h
            off_w = 2 - tap_w if flipped else tap_w
            window = extended[
                start_t : start_t + frames, off_h : off_h + height, off_w : off_w + breadth
            ]
            pieces.append(window.reshape(-1, extended.shape[-1]))
    return jnp.concatenate(pieces, axis=1)


def forward_taps(extended, filters, frames, height, breadth):
    channels = filters.shape[-1]
    running = jnp.zeros((frames * height * breadth, channels), jnp.float32)
    for tap_t in range(3):
        columns = plane_columns(extended, tap_t, False, frames, height, breadth)
        block = filters[9 * tap_t : 9 * tap_t + 9].reshape(9 * channels, channels)
        running = running + jnp.dot(columns, block, precision=HIGHEST)
    return running.reshape(frames, height, breadth, channels)


def transpose_taps(extended, filters, frames, height, breadth):
    channels = filters.shape[1]
    running = jnp.zeros((frames * height * breadth, channels), jnp.float32)
    for tap_t in range(3):
        columns = plane_columns(extended, 2 - tap_t, True, frames, height, breadth)
        block = jnp.transpose(filters[9 * tap_t : 9 * tap_t + 9], (0, 2, 1)).reshape(
            9 * channels, channels
        )
        running = running + jnp.dot(columns, block, precision=HIGHEST)
    return running.reshape(frames, height, breadth, channels)


def weight_taps(extended, cotangent):
    frames, height, breadth, channels = cotangent.shape
    flat_cot = cotangent.reshape(-1, channels)
    pieces = []
    for tap_t in range(3):
        columns = plane_columns(extended, tap_t, False, frames, height, breadth)
        pieces.append(
            lax.dot_general(columns, flat_cot, (((0,), (0,)), ((), ())), precision=HIGHEST)
        )
    return jnp.concatenate(pieces, axis=0)


def per_device(video_in, first_filter, first_bias, second_filter, grad_output):
    frames, height, breadth, channels = video_in.shape
    earlier = passed_along(video_in[frames - 2 :], "ta", 1)
    input_ext = extended_2(jnp.concatenate([earlier, video_in], axis=0), (("ha", 1), ("wa", 2)), 1)
    pre = forward_taps(input_ext, first_filter, frames, height, breadth) + first_bias
    act = jax.nn.silu(pre)
    act_before = passed_along(act[frames - 2 :], "ta", 1)
    act_ext = extended_2(jnp.concatenate([act_before, act], axis=0), (("ha", 1), ("wa", 2)), 1)
    later = passed_along(grad_output[:2], "ta", -1)
    cot_ext = extended_2(jnp.concatenate([grad_output, later], axis=0), (("ha", 1), ("wa", 2)), 1)
    raw_second = weight_taps(act_ext, grad_output)
    grad_act = transpose_taps(cot_ext, second_filter, frames, height, breadth)
    sigmoid_pre = jax.nn.sigmoid(pre)
    grad_pre = grad_act * sigmoid_pre * (1.0 + pre * (1.0 - sigmoid_pre))
    raw_bias = jnp.sum(grad_pre.reshape(-1, channels), axis=0)
    raw_first = weight_taps(input_ext, grad_pre)
    grad_later = passed_along(grad_pre[:2], "ta", -1)
    grad_ext = extended_2(
        jnp.concatenate([grad_pre, grad_later], axis=0), (("ha", 1), ("wa", 2)), 1
    )
    grad_input = transpose_taps(grad_ext, first_filter, frames, height, breadth)
    plane_first, plane_second, plane_bias = lax.psum(
        (raw_first, raw_second, raw_bias), ("ha", "wa")
    )
    share_first, share_second = (
        lax.psum_scatter(plane_first, "ta", scatter_dimension=0, tiled=True),
        lax.psum_scatter(plane_second, "ta", scatter_dimension=0, tiled=True),
    )
    share_squares = jnp.sum(share_first * share_first) + jnp.sum(share_second * share_second)
    filter_squares, bias_total = lax.psum((share_squares, plane_bias), "ta")
    squares = filter_squares + jnp.sum(bias_total * bias_total)
    limit = jnp.sqrt(jnp.float32(54 * channels * channels + channels))
    factor = jnp.minimum(jnp.float32(1.0), limit / jnp.sqrt(squares))
    return (grad_input, factor * share_first, factor * share_second, factor * bias_total)


def solution(mesh):
    placed = (P("ta", "ha", "wa", None), P(), P(), P(), P("ta", "ha", "wa", None))
    return jax.shard_map(
        per_device,
        mesh=mesh,
        in_specs=placed,
        out_specs=(P("ta", "ha", "wa", None), P("ta", None), P("ta", None), P()),
        check_vma=False,
    )
```

profile of v0, /device:TPU:1, one launch (start us, length us, event | category | flops | bytes accessed | tf_op | source)
XLA Modules:
  0.0 405.0 jit_solution(15341307018993965455)
XLA Ops:
  8.1 3.3 collective-permute-start
  12.4 4.8 %collective-permute-start.5 = (f32[2,8,16,128]{3,2,1,0:T(8,128)S(1)}, f32[2,8,16,128]{3,2,1,0:T(8,128)S(1)}, u32[]{:S(2)}, u32[]{:S(2)}) collective-permute-start(f32[2,8,16,128]{3,2,1,0:T(8,128)S(1)} %slice.549), channel_id=1, source_target_pairs={{0,8},{8,16},{16,24},{24,32},{32,40},{40,48},{48,56},{56,64},{64,7... | collective-permute-start | bytes 393224 | tf_op jit(solution)/shard_map/ppermute | solution.py:12
  17.2 3.4 slice_bitcast_fusion
  28.4 4.0 collective-permute-start.6
  35.1 4.0 collective-permute-start.4
  39.2 3.2 collective-permute-start.8
  60.1 14.0 %convolution_add_fusion.3 = f32[512,128]{1,0:T(8,128)S(1)} fusion(f32[512,128]{1,0:T(8,128)S(1)} %fusion.28, f32[512,1152]{1,0:T(8,128)S(1)} %constant_dynamic-update-slice_fusion.40, f32[1152,128]{1,0:T(8,128)S(1)} %bitcast.172), kind=kOutput, calls=%fused_computation.5 | convolution fusion | flops 906035200 | bytes 3473408 | tf_op jit(solution)/shard_map/dot_general | solution.py:47
  77.1 4.8 %collective-permute-start.15 = (f32[2,8,16,128]{3,2,1,0:T(8,128)}, f32[2,8,16,128]{3,2,1,0:T(8,128)S(1)}, u32[]{:S(2)}, u32[]{:S(2)}) collective-permute-start(f32[2,8,16,128]{3,2,1,0:T(8,128)} %slice.732), channel_id=1, source_target_pairs={{0,8},{8,16},{16,24},{24,32},{32,40},{40,48},{48,56},{56,64},{64,7... | collective-permute-start | bytes 393224 | tf_op jit(solution)/shard_map/ppermute | solution.py:12
  90.9 3.8 collective-permute-start.16
  96.0 4.0 collective-permute-start.11
  110.0 5.2 %collective-permute-start.14 = (f32[6,10,1,128]{3,2,1,0:T(1,128)S(1)}, f32[6,10,1,128]{3,2,1,0:T(1,128)}, u32[]{:S(2)}, u32[]{:S(2)}) collective-permute-start(f32[6,10,1,128]{3,2,1,0:T(1,128)S(1)} %get-tuple-element.97), channel_id=1, source_target_pairs={{0,1},{1,2},{2,3},{4,5},{5,6},{6,7},{8,9},{9,10},{10,11},{12,13},{... | collective-permute-start | bytes 92168 | tf_op jit(solution)/shard_map/ppermute | solution.py:20
  117.0 3.9 fusion.33
  121.2 3.9 fusion.34
  126.1 4.3 %fusion.35 = f32[1152,128]{1,0:T(8,128)S(1)} fusion(f32[512,1152]{1,0:T(8,128)S(1)} %constant_dynamic-update-slice_fusion.103, f32[512,128]{1,0:T(8,128)S(1)} %bitcast.164), kind=kOutput, calls=%fused_computation.224 | convolution fusion | flops 905969664 | bytes 3211264 | tf_op jit(solution)/shard_map/dot_general | solution.py:70
  134.2 14.2 %psum.38 = f32[128]{0:T(128)S(1)} all-reduce(f32[128]{0:T(128)S(1)} %get-tuple-element.8), channel_id=1, replica_groups=mesh['ta'=16,'ha'=2,'wa'=4] {'ha','wa'}, use_global_device_ids=true, to_apply=%region_8.9 | all-reduce | flops 128 | bytes 1024 | tf_op jit(solution)/shard_map/psum | solution.py:96
  158.0 3.9 fusion.30
  161.8 3.9 fusion.31
  165.7 3.9 fusion.32
  182.9 21.3 %reduce-scatter.9.cloned.1.call-done = f32[216,128]{1,0:T(8,128)} async-done(((f32[3456,128]{1,0:T(8,128)}), f32[216,128]{1,0:T(8,128)}) %reduce-scatter.9.cloned.1.call-update) | async-done | bytes 110608
  204.2 72.4 %reduce-scatter.7.cloned.1.call-done = f32[216,128]{1,0:T(8,128)} async-done(((f32[3456,128]{1,0:T(8,128)}), f32[216,128]{1,0:T(8,128)}) %reduce-scatter.7.cloned.1.call-update) | async-done | bytes 110608
  276.6 3.7 convolution_add_fusion.1
  280.3 66.8 %all-reduce.6.cloned.1.call-done = (f32[216,128]{1,0:T(8,128)}, f32[216,128]{1,0:T(8,128)}) async-done(((f32[216,128]{1,0:T(8,128)}, f32[216,128]{1,0:T(8,128)}), (f32[216,128]{1,0:T(8,128)}, f32[216,128]{1,0:T(8,128)})) %all-reduce.6.cloned.1.call-update) | async-done | bytes 221200 | tf_op jit(solution)/shard_map/psum | solution.py:96
  351.6 4.4 %convolution_add_fusion = f32[512,128]{1,0:T(8,128)} fusion(f32[512,128]{1,0:T(8,128)} %convolution_add_fusion.1, f32[512,1152]{1,0:T(8,128)} %constant_dynamic-update-slice_fusion.76, f32[1152,128]{1,0:T(8,128)S(1)} %bitcast.165), kind=kOutput, calls=%fused_computation.2 | convolution fusion | flops 906035200 | bytes 3473408 | tf_op jit(solution)/shard_map/dot_general | solution.py:59
  356.0 38.6 %all-reduce.2 = (f32[]{:T(128)}, f32[128]{0:T(128)S(1)}) all-reduce(f32[]{:T(128)S(6)} %add.81, f32[128]{0:T(128)S(1)} %psum.38), channel_id=1, replica_groups=mesh['ta'=16,'ha'=2,'wa'=4] {'ta'}, use_global_device_ids=true, to_apply=%region_6.7 | all-reduce | flops 129 | bytes 1032 | tf_op jit(solution)/shard_map/psum | solution.py:104
  (291 shorter events, 87.2 us)
Async XLA Ops:
  7.2 197.0 %reduce-scatter.9.cloned.1.call-start = ((), (), s32[]{:S(2)}) async-start(), calls=%async_computation.3 | async-start | bytes 1880064
  8.1 15.8 %collective-permute-start = (f32[2,8,16,128]{3,2,1,0:T(8,128)S(1)}, f32[2,8,16,128]{3,2,1,0:T(8,128)S(1)}, u32[]{:S(2)}, u32[]{:S(2)}) collective-permute-start(f32[2,8,16,128]{3,2,1,0:T(8,128)S(1)} %slice.515), channel_id=1, source_target_pairs={{8,0},{16,8},{24,16},{32,24},{40,32},{48,40},{56,48},{64,56},{72,6... | collective-permute-start | bytes 393224 | tf_op jit(solution)/shard_map/ppermute | solution.py:12
  12.4 15.9 %collective-permute-start.5 = (f32[2,8,16,128]{3,2,1,0:T(8,128)S(1)}, f32[2,8,16,128]{3,2,1,0:T(8,128)S(1)}, u32[]{:S(2)}, u32[]{:S(2)}) collective-permute-start(f32[2,8,16,128]{3,2,1,0:T(8,128)S(1)} %slice.549), channel_id=1, source_target_pairs={{0,8},{8,16},{16,24},{24,32},{32,40},{40,48},{48,56},{56,64},{64,7... | collective-permute-start | bytes 393224 | tf_op jit(solution)/shard_map/ppermute | solution.py:12
  24.0 9.7 %collective-permute-start.1 = (f32[6,1,16,128]{3,2,1,0:T(8,128)S(1)}, f32[6,1,16,128]{3,2,1,0:T(8,128)S(1)}, u32[]{:S(2)}, u32[]{:S(2)}) collective-permute-start(f32[6,1,16,128]{3,2,1,0:T(8,128)S(1)} %get-tuple-element.155), channel_id=1, source_target_pairs={{0,4},{1,5},{2,6},{3,7},{8,12},{9,13},{10,14},{11,15},{16,20},{17,... | collective-permute-start | bytes 147464 | tf_op jit(solution)/shard_map/ppermute | solution.py:20
  27.0 6.7 %collective-permute-start.2 = (f32[6,1,16,128]{3,2,1,0:T(8,128)S(1)}, f32[6,1,16,128]{3,2,1,0:T(8,128)S(1)}, u32[]{:S(2)}, u32[]{:S(2)}) collective-permute-start(f32[6,1,16,128]{3,2,1,0:T(8,128)S(1)} %get-tuple-element.156), channel_id=1, source_target_pairs={{4,0},{5,1},{6,2},{7,3},{12,8},{13,9},{14,10},{15,11},{20,16},{21,... | collective-permute-start | bytes 147464 | tf_op jit(solution)/shard_map/ppermute | solution.py:23
  28.4 10.7 %collective-permute-start.6 = (f32[6,1,16,128]{3,2,1,0:T(8,128)S(1)}, f32[6,1,16,128]{3,2,1,0:T(8,128)S(1)}, u32[]{:S(2)}, u32[]{:S(2)}) collective-permute-start(f32[6,1,16,128]{3,2,1,0:T(8,128)S(1)} %get-tuple-element.148), channel_id=1, source_target_pairs={{0,4},{1,5},{2,6},{3,7},{8,12},{9,13},{10,14},{11,15},{16,20},{17,... | collective-permute-start | bytes 147464 | tf_op jit(solution)/shard_map/ppermute | solution.py:20
  32.4 6.7 %collective-permute-start.7 = (f32[6,1,16,128]{3,2,1,0:T(8,128)S(1)}, f32[6,1,16,128]{3,2,1,0:T(8,128)S(1)}, u32[]{:S(2)}, u32[]{:S(2)}) collective-permute-start(f32[6,1,16,128]{3,2,1,0:T(8,128)S(1)} %get-tuple-element.149), channel_id=1, source_target_pairs={{4,0},{5,1},{6,2},{7,3},{12,8},{13,9},{14,10},{15,11},{20,16},{21,... | collective-permute-start | bytes 147464 | tf_op jit(solution)/shard_map/ppermute | solution.py:23
  33.8 10.3 %collective-permute-start.3 = (f32[6,10,1,128]{3,2,1,0:T(1,128)S(1)}, f32[6,10,1,128]{3,2,1,0:T(1,128)S(1)}, u32[]{:S(2)}, u32[]{:S(2)}) collective-permute-start(f32[6,10,1,128]{3,2,1,0:T(1,128)S(1)} %get-tuple-element.106), channel_id=1, source_target_pairs={{1,0},{2,1},{3,2},{5,4},{6,5},{7,6},{9,8},{10,9},{11,10},{13,12},{... | collective-permute-start | bytes 92168 | tf_op jit(solution)/shard_map/ppermute | solution.py:23
  35.1 9.0 %collective-permute-start.4 = (f32[6,10,1,128]{3,2,1,0:T(1,128)S(1)}, f32[6,10,1,128]{3,2,1,0:T(1,128)S(1)}, u32[]{:S(2)}, u32[]{:S(2)}) collective-permute-start(f32[6,10,1,128]{3,2,1,0:T(1,128)S(1)} %get-tuple-element.105), channel_id=1, source_target_pairs={{0,1},{1,2},{2,3},{4,5},{5,6},{6,7},{8,9},{9,10},{10,11},{12,13},{... | collective-permute-start | bytes 92168 | tf_op jit(solution)/shard_map/ppermute | solution.py:20
  39.2 5.6 %collective-permute-start.8 = (f32[6,10,1,128]{3,2,1,0:T(1,128)S(1)}, f32[6,10,1,128]{3,2,1,0:T(1,128)S(1)}, u32[]{:S(2)}, u32[]{:S(2)}) collective-permute-start(f32[6,10,1,128]{3,2,1,0:T(1,128)S(1)} %get-tuple-element.102), channel_id=1, source_target_pairs={{0,1},{1,2},{2,3},{4,5},{5,6},{6,7},{8,9},{9,10},{10,11},{12,13},{... | collective-permute-start | bytes 92168 | tf_op jit(solution)/shard_map/ppermute | solution.py:20
  42.4 5.2 %collective-permute-start.9 = (f32[6,10,1,128]{3,2,1,0:T(1,128)S(1)}, f32[6,10,1,128]{3,2,1,0:T(1,128)S(1)}, u32[]{:S(2)}, u32[]{:S(2)}) collective-permute-start(f32[6,10,1,128]{3,2,1,0:T(1,128)S(1)} %get-tuple-element.101), channel_id=1, source_target_pairs={{1,0},{2,1},{3,2},{5,4},{6,5},{7,6},{9,8},{10,9},{11,10},{13,12},{... | collective-permute-start | bytes 92168 | tf_op jit(solution)/shard_map/ppermute | solution.py:23
  77.1 13.8 %collective-permute-start.15 = (f32[2,8,16,128]{3,2,1,0:T(8,128)}, f32[2,8,16,128]{3,2,1,0:T(8,128)S(1)}, u32[]{:S(2)}, u32[]{:S(2)}) collective-permute-start(f32[2,8,16,128]{3,2,1,0:T(8,128)} %slice.732), channel_id=1, source_target_pairs={{0,8},{8,16},{16,24},{24,32},{32,40},{40,48},{48,56},{56,64},{64,7... | collective-permute-start | bytes 393224 | tf_op jit(solution)/shard_map/ppermute | solution.py:12
  82.6 13.4 %collective-permute-start.10 = (f32[2,8,16,128]{3,2,1,0:T(8,128)}, f32[2,8,16,128]{3,2,1,0:T(8,128)S(1)}, u32[]{:S(2)}, u32[]{:S(2)}) collective-permute-start(f32[2,8,16,128]{3,2,1,0:T(8,128)} %slice.705), channel_id=1, source_target_pairs={{8,0},{16,8},{24,16},{32,24},{40,32},{48,40},{56,48},{64,56},{72,6... | collective-permute-start | bytes 393224 | tf_op jit(solution)/shard_map/ppermute | solution.py:12
  90.9 11.3 %collective-permute-start.16 = (f32[6,1,16,128]{3,2,1,0:T(8,128)S(1)}, f32[6,1,16,128]{3,2,1,0:T(8,128)S(1)}, u32[]{:S(2)}, u32[]{:S(2)}) collective-permute-start(f32[6,1,16,128]{3,2,1,0:T(8,128)S(1)} %get-tuple-element.135), channel_id=1, source_target_pairs={{0,4},{1,5},{2,6},{3,7},{8,12},{9,13},{10,14},{11,15},{16,20},{17,... | collective-permute-start | bytes 147464 | tf_op jit(solution)/shard_map/ppermute | solution.py:20
  94.7 7.5 %collective-permute-start.17 = (f32[6,1,16,128]{3,2,1,0:T(8,128)S(1)}, f32[6,1,16,128]{3,2,1,0:T(8,128)S(1)}, u32[]{:S(2)}, u32[]{:S(2)}) collective-permute-start(f32[6,1,16,128]{3,2,1,0:T(8,128)S(1)} %get-tuple-element.136), channel_id=1, source_target_pairs={{4,0},{5,1},{6,2},{7,3},{12,8},{13,9},{14,10},{15,11},{20,16},{21,... | collective-permute-start | bytes 147464 | tf_op jit(solution)/shard_map/ppermute | solution.py:23
  96.0 11.0 %collective-permute-start.11 = (f32[6,1,16,128]{3,2,1,0:T(8,128)S(1)}, f32[6,1,16,128]{3,2,1,0:T(8,128)S(1)}, u32[]{:S(2)}, u32[]{:S(2)}) collective-permute-start(f32[6,1,16,128]{3,2,1,0:T(8,128)S(1)} %get-tuple-element.141), channel_id=1, source_target_pairs={{0,4},{1,5},{2,6},{3,7},{8,12},{9,13},{10,14},{11,15},{16,20},{17,... | collective-permute-start | bytes 147464 | tf_op jit(solution)/shard_map/ppermute | solution.py:20
  100.0 7.0 %collective-permute-start.12 = (f32[6,1,16,128]{3,2,1,0:T(8,128)S(1)}, f32[6,1,16,128]{3,2,1,0:T(8,128)S(1)}, u32[]{:S(2)}, u32[]{:S(2)}) collective-permute-start(f32[6,1,16,128]{3,2,1,0:T(8,128)S(1)} %get-tuple-element.142), channel_id=1, source_target_pairs={{4,0},{5,1},{6,2},{7,3},{12,8},{13,9},{14,10},{15,11},{20,16},{21,... | collective-permute-start | bytes 147464 | tf_op jit(solution)/shard_map/ppermute | solution.py:23
  102.4 13.8 %collective-permute-start.18 = (f32[6,10,1,128]{3,2,1,0:T(1,128)S(1)}, f32[6,10,1,128]{3,2,1,0:T(1,128)S(1)}, u32[]{:S(2)}, u32[]{:S(2)}) collective-permute-start(f32[6,10,1,128]{3,2,1,0:T(1,128)S(1)} %get-tuple-element.94), channel_id=1, source_target_pairs={{0,1},{1,2},{2,3},{4,5},{5,6},{6,7},{8,9},{9,10},{10,11},{12,13},{... | collective-permute-start | bytes 92168 | tf_op jit(solution)/shard_map/ppermute | solution.py:20
  105.6 10.6 %collective-permute-start.19 = (f32[6,10,1,128]{3,2,1,0:T(1,128)S(1)}, f32[6,10,1,128]{3,2,1,0:T(1,128)S(1)}, u32[]{:S(2)}, u32[]{:S(2)}) collective-permute-start(f32[6,10,1,128]{3,2,1,0:T(1,128)S(1)} %get-tuple-element.93), channel_id=1, source_target_pairs={{1,0},{2,1},{3,2},{5,4},{6,5},{7,6},{9,8},{10,9},{11,10},{13,12},{... | collective-permute-start | bytes 92168 | tf_op jit(solution)/shard_map/ppermute | solution.py:23
  108.7 23.1 %collective-permute-start.13 = (f32[6,10,1,128]{3,2,1,0:T(1,128)}, f32[6,10,1,128]{3,2,1,0:T(1,128)}, u32[]{:S(2)}, u32[]{:S(2)}) collective-permute-start(f32[6,10,1,128]{3,2,1,0:T(1,128)} %get-tuple-element.98), channel_id=1, source_target_pairs={{1,0},{2,1},{3,2},{5,4},{6,5},{7,6},{9,8},{10,9},{11,10},{13,12},{... | collective-permute-start | bytes 92168 | tf_op jit(solution)/shard_map/ppermute | solution.py:23
  110.0 21.8 %collective-permute-start.14 = (f32[6,10,1,128]{3,2,1,0:T(1,128)S(1)}, f32[6,10,1,128]{3,2,1,0:T(1,128)}, u32[]{:S(2)}, u32[]{:S(2)}) collective-permute-start(f32[6,10,1,128]{3,2,1,0:T(1,128)S(1)} %get-tuple-element.97), channel_id=1, source_target_pairs={{0,1},{1,2},{2,3},{4,5},{5,6},{6,7},{8,9},{9,10},{10,11},{12,13},{... | collective-permute-start | bytes 92168 | tf_op jit(solution)/shard_map/ppermute | solution.py:20
  131.8 144.8 %reduce-scatter.7.cloned.1.call-start = ((), (), s32[]{:S(2)}) async-start(), calls=%async_computation.2 | async-start | bytes 1880064
  171.0 176.1 %all-reduce.6.cloned.1.call-start = ((), (), s32[]{:S(2)}) async-start(), calls=%async_computation.4 | async-start | bytes 442368 | tf_op jit(solution)/shard_map/psum | solution.py:96
  182.9 168.7 %copy-start.8 = (f32[9,128,128]{2,1,0:T(8,128)S(1)}, f32[9,128,128]{2,1,0:T(8,128)}, u32[]{:S(2)}) copy-start(f32[9,128,128]{2,1,0:T(8,128)} %copy.26) | copy-start | bytes 1769476
  (43 other events, 400.5 us)
Sparse Core Ops, SparseCore 0:
  131.9 72.2 reduce-scatter.8
  208.2 68.3 reduce-scatter.6
  279.2 67.9 all-reduce.5
where the time goes:
time: 410 us; the launch traced here: 405 us
  waiting for transfers between devices  163 us (40%)
  matrix products  59 us (14%)
  starting transfers between devices  55.9 us (14%)
  blocking collectives  52.8 us (13%)
  local copies, waits for them, and re-layouts  42.9 us (10%)
  between operations  18.3 us (4%)
  other arithmetic  12.7 us (3%)
    unnamed x5, waiting for transfers between devices  93.8 us
    psum x1, waiting for transfers between devices, per_device(): lax.psum((raw_first, raw_second, raw_bias), ('ha', 'wa'))  66.8 us
    psum x1, blocking collectives, per_device(): filter_squares, bias_total = lax.psum((share_squares, plane_bias), 'ta')  38.6 us
    ppermute x8, starting transfers between devices, extended_2(): lax.ppermute(lax.slice_in_dim(block, block.shape[dim] - width, None, axis...  30.4 us
    dot_general x6, matrix products, weight_taps(): lax.dot_general(columns, flat_cot, (((0,), (0,)), ((), ())), precision=HI...  23.6 us
    unnamed x188, local copies, waits for them, and re-layouts  21.7 us
    dot_general x3, matrix products, forward_taps(): running = running + jnp.dot(columns, block, precision=HIGHEST)  18.2 us
    dot_general x6, matrix products, transpose_taps(): running = running + jnp.dot(columns, block, precision=HIGHEST)  17.2 us
  transfers between devices with their start and end apart: 23, of which 4 were waited for; matrix products, arithmetic and copies ran while one was open for 18% of the time, Pallas kernels for 0%

commit v1 on v0

v1 whole, which is shorter than its diff:
```python
import jax
import jax.numpy as jnp
from jax import lax
from jax.experimental import pallas as pl
from jax.experimental.pallas import tpu as pltpu
from jax.sharding import PartitionSpec as P

f32, bf16 = jnp.float32, jnp.bfloat16
MESH = pl.DeviceIdType.MESH
C = 128
T, H, W = 4, 8, 16
V = T * H * W
ROWS = 27 * C
OWN = ROWS // 16
PAD = OWN + 8
HALF = PAD // 2
QUART = HALF // 2
LEFT = 8
LIMIT = float(54 * C * C + C)


def split(value):
    high = value.astype(bf16)
    low = (value - high.astype(f32)).astype(bf16)
    return high, low


def mod(value, count):
    return lax.rem(value + 2 * count, count)


def rows8(start, size):
    return pl.ds(pl.multiple_of(start, 8), size)


def remote(src, dst, send, recv, device):
    return pltpu.make_async_remote_copy(
        src_ref=src, dst_ref=dst, send_sem=send, recv_sem=recv, device_id=device,
        device_id_type=MESH,
    )


def kernel(
    video, first, bias, second, cot,
    grad_input, grad_first, grad_second, grad_bias,
    w_f32, w_split, ext, cols, cols_ext, shifted, acc, pre_ref, act_t, vid_t,
    raw, bias8, pack, core0, core1, rs1_0, rs1_1, rs2_0, rs2_1,
    tot, x_recv, tot2, tot3, full, note, notes,
    local_sem, halo_send, halo_recv, core_send, core_recv, rs_send, rs_recv,
    x_send, x_rcv, ag_send, ag_recv, n_send, n_recv,
):
    ta, ha, wa = lax.axis_index("ta"), lax.axis_index("ha"), lax.axis_index("wa")
    core = lax.rem(ta, 2)
    x_hi = lax.rem(ta // 2, 2)
    z = ta // 4
    y = wa
    other = 1 - ha

    own_at = (2, 0, 0)
    blocks = [
        pltpu.make_async_copy(
            src, ext.at[n, pl.ds(own_at[n], T), pl.ds(1, H), pl.ds(LEFT, W)], local_sem.at[n]
        )
        for n, src in enumerate((video, cot))
    ]
    loads = [
        pltpu.make_async_copy(src, w_f32.at[n], local_sem.at[2 + n])
        for n, src in enumerate((first, second))
    ]
    for copy in blocks + loads:
        copy.start()

    gap = 9 * ha
    for n in range(3):
        ext[n, :, pl.ds(gap, 1)] = jnp.zeros((T + 2, 1, 32, C), f32)
        cols_ext[n, :, :, pl.ds(gap, 1)] = jnp.zeros((2, T + 2, 1, 1, C), f32)

    barrier = pltpu.get_barrier_semaphore()
    greeted = []
    for dt in (-1, 0, 1):
        for row in (ha, other):
            for dw in (-1, 0, 1):
                if not (dt == 0 and row is ha and dw == 0):
                    greeted.append((mod(ta + dt, 16), row, mod(wa + dw, 4)))
    for step in range(2, 15):
        greeted.append((mod(ta + step, 16), ha, wa))
    greeted.append((ta, ha, mod(wa + 2, 4)))
    flip2 = ta + 2 - 4 * x_hi
    greeted.append((flip2, other, wa))
    for device in greeted:
        pl.semaphore_signal(barrier, inc=1, device_id=device, device_id_type=MESH)
    pl.semaphore_wait(barrier, len(greeted))

    halo_at = (0, 4, 4)
    edge_at = (2, 0, 0)
    along = (1, -1, -1)
    edge_row = 7 * other

    def halo_plain(n, src):
        copies = []
        for slot, (dt, dh) in enumerate(((0, 1), (1, 0), (1, 1))):
            frames = pl.ds(edge_at[n], 2) if dt else pl.ds(0, T)
            to = pl.ds(halo_at[n], 2) if dt else pl.ds(own_at[n], T)
            rows = pl.ds(edge_row, 1) if dh else pl.ds(0, H)
            to_rows = pl.ds(gap, 1) if dh else pl.ds(1, H)
            copies.append(
                remote(
                    src(frames, rows),
                    ext.at[n, to, to_rows, pl.ds(LEFT, W)],
                    halo_send.at[n, slot], halo_recv.at[n, slot],
                    (mod(ta + along[n] * dt, 16), other if dh else ha, wa),
                )
            )
        return copies

    def halo_columns(n):
        copies = []
        slot = 3
        for dt in (0, 1):
            for dh in (0, 1):
                for side, dw in ((0, -1), (1, 1)):
                    if dt + dh + abs(dw) == 0:
                        continue
                    frames = pl.ds(edge_at[n], 2) if dt else pl.ds(0, T)
                    to = pl.ds(halo_at[n], 2) if dt else pl.ds(own_at[n], T)
                    rows = pl.ds(edge_row, 1) if dh else pl.ds(0, H)
                    to_rows = pl.ds(gap, 1) if dh else pl.ds(1, H)
                    copies.append(
                        remote(
                            cols.at[n, side, frames, rows],
                            cols_ext.at[n, 1 - side, to, to_rows],
                            halo_send.at[n, slot], halo_recv.at[n, slot],
                            (mod(ta + along[n] * dt, 16), other if dh else ha, mod(wa + dw, 4)),
                        )
                    )
                    slot += 1
        return copies

    def pack_columns(n):
        own = ext[n, pl.ds(own_at[n], T), pl.ds(1, H), pl.ds(LEFT, W)]
        cols[n, 0] = own[:, :, 0:1]
        cols[n, 1] = own[:, :, W - 1 : W]

    plain = [halo_plain(0, lambda t, h: video.at[t, h]), halo_plain(1, lambda t, h: cot.at[t, h])]
    for copies in plain:
        for copy in copies:
            copy.start()
    strips = [halo_columns(0), halo_columns(1)]
    for n in (0, 1):
        blocks[n].wait()
        pack_columns(n)
        for copy in strips[n]:
            copy.start()

    for copy in loads:
        copy.wait()

    def split_filters(tap, _):
        for n in range(2):
            high, low = split(w_f32[n, tap])
            w_split[n, tap, :, :C] = high
            w_split[n, tap, :, C:] = low
        return 0

    lax.fori_loop(0, 27, split_filters, 0)

    def transposed(value, ref):
        high, low = split(value.T)
        ref[:C] = high
        ref[C:] = low

    transposed(ext[0, pl.ds(2, T), pl.ds(1, H), pl.ds(LEFT, W)].reshape(V, C), vid_t)

    left_in = (wa > 0).astype(f32)
    right_in = (wa < 3).astype(f32)
    frame_in = ((ta > 0).astype(f32), (ta < 15).astype(f32), (ta < 15).astype(f32))

    def shift_columns(n):
        def frame(t, _):
            ext[n, t, :, LEFT - 1 : LEFT] = cols_ext[n, 0, t] * left_in
            ext[n, t, :, LEFT + W : LEFT + W + 1] = cols_ext[n, 1, t] * right_in
            is_halo = jnp.logical_and(t >= halo_at[n], t < halo_at[n] + 2)
            keep = jnp.where(is_halo, frame_in[n], 1.0)
            for c in range(3):
                high, low = split(ext[n, t, :, LEFT - 1 + c : LEFT - 1 + c + W] * keep)
                shifted[n, c, t, :, :, :C] = high
                shifted[n, c, t, :, :, C:] = low
            return 0

        lax.fori_loop(0, T + 2, frame, 0)

    def conv(n, filters, back):
        for a in range(3):
            pieces, blocks_w = [], []
            for b in range(3):
                for c in range(3):
                    at = (2 - a, 2 - b, 2 - c) if back else (a, b, c)
                    window = shifted[n, at[2], pl.ds(at[0], T), pl.ds(at[1], H)]
                    pieces.append(window.reshape(V, 2 * C))
                    w = w_split[filters, 9 * a + 3 * b + c]
                    if back:
                        high, low = w[:, :C], w[:, C:]
                        blocks_w.append(
                            jnp.concatenate(
                                [
                                    jnp.concatenate([high, high], axis=1),
                                    jnp.concatenate([low, low], axis=1),
                                ],
                                axis=0,
                            )
                        )
                    else:
                        blocks_w += [w, w]
            columns = jnp.concatenate(pieces, axis=1)
            if back:
                product = lax.dot_general(
                    columns, jnp.concatenate(blocks_w, axis=1), (((1,), (1,)), ((), ())),
                    preferred_element_type=f32,
                )
            else:
                product = jnp.dot(
                    columns, jnp.concatenate(blocks_w, axis=0), preferred_element_type=f32
                )
            if a == 0:
                acc[...] = product
            else:
                acc[...] += product
        return acc[:, :C] + acc[:, C:]

    def weight_grad(fixed, n, f):
        def taps(step, _):
            a, b = step // 3, lax.rem(step, 3)
            for c in range(3):
                window = shifted[n, 2 - c, pl.ds(2 - a, T), pl.ds(2 - b, H)].reshape(V, 2 * C)
                o = jnp.dot(fixed[...], window, preferred_element_type=f32)
                raw[f, rows8((3 * step + c) * C, C)] = (o[:C, :C] + o[C:, :C]) + (
                    o[:C, C:] + o[C:, C:]
                )
            return 0

        lax.fori_loop(0, 9, taps, 0)

    for copy in plain[0] + strips[0]:
        copy.wait_recv()
    shift_columns(0)
    pre = conv(0, 0, False) + bias[...]
    pre_ref[...] = pre
    sig = 1.0 / (1.0 + jnp.exp(-pre))
    transposed(pre * sig, act_t)

    for copy in plain[1] + strips[1]:
        copy.wait_recv()
    shift_columns(1)
    grad_act = conv(1, 1, True)
    pre = pre_ref[...]
    sig = 1.0 / (1.0 + jnp.exp(-pre))
    grad_pre = grad_act * sig * (1.0 + pre * (1.0 - sig))
    bias8[...] = jnp.sum(grad_pre.reshape(V // 8, 8, C), axis=0)
    ext[2, pl.ds(0, T), pl.ds(1, H), pl.ds(LEFT, W)] = grad_pre.reshape(T, H, W, C)
    plain.append(
        halo_plain(2, lambda t, h: ext.at[2, t, pl.ds(h.start + 1, h.size), pl.ds(LEFT, W)])
    )
    for copy in plain[2]:
        copy.start()
    pack_columns(2)
    strips.append(halo_columns(2))
    for copy in strips[2]:
        copy.start()

    core_buf = (core0, core1)

    def owner(f, i, j):
        kz, kx = (i, j) if f == 0 else (j, i)
        return 4 * kz + 2 * kx

    def core_swap(f):
        outer, inner = (4, 2) if f == 0 else (2, 4)
        for i in range(outer):
            for j in range(inner):
                k = owner(f, i, j) + 1 - core
                pack[f, i * inner + j, :OWN] = raw[f, rows8(OWN * k, OWN)]
                pack[f, i * inner + j, OWN:] = bias8[...] if f else jnp.zeros((8, C), f32)
        copy = remote(
            pack.at[f], core_buf[f], core_send.at[f], core_recv.at[f],
            (ta + 1 - 2 * core, ha, wa),
        )
        copy.start()
        return copy

    def core_add(f):
        outer, inner = (4, 2) if f == 0 else (2, 4)
        for i in range(outer):
            for j in range(inner):
                k = owner(f, i, j) + core
                q = i * inner + j
                core_buf[f][q, :OWN] += raw[f, rows8(OWN * k, OWN)]
                if f:
                    core_buf[f][q, OWN:] += bias8[...]

    weight_grad(act_t, 1, 0)
    swap0 = core_swap(0)
    for copy in plain[2] + strips[2]:
        copy.wait_recv()
    shift_columns(2)
    weight_grad(vid_t, 2, 1)
    swap1 = core_swap(1)

    z_next, z_prev = (mod(ta + 4, 16), ha, wa), (mod(ta - 4, 16), ha, wa)
    y_next, y_prev = (ta, ha, mod(wa + 1, 4)), (ta, ha, mod(wa - 1, 4))

    def ring_start(s, i, nxt, prv, part, recv):
        copies = []
        for slot, (shard, half, device) in enumerate(
            ((2, 0, nxt), (1, 1, nxt), (2, 1, prv), (-1, 0, prv))
        ):
            copies.append(
                remote(
                    part(mod(i + shard, 4), half), recv.at[slot],
                    rs_send.at[s, slot], rs_recv.at[s, slot], device,
                )
            )
        for copy in copies:
            copy.start()
        return copies

    def ring_middle(s, i, nxt, prv, part, recv, copies):
        for slot, shard, half, device in ((0, 1, 0, nxt), (2, -1, 1, prv)):
            copies[slot].wait_recv()
            mine = part(mod(i + shard, 4), half)
            mine[...] += recv[slot]
            copy = remote(
                mine, recv.at[4 + slot // 2],
                rs_send.at[s, 4 + slot // 2], rs_recv.at[s, 4 + slot // 2], device,
            )
            copy.start()
            copies.append(copy)

    def ring_end(i, part, recv, copies, stores):
        for half, one, two in ((0, 3, 4), (1, 1, 5)):
            copies[one].wait_recv()
            copies[two].wait_recv()
            stores[half][...] = part(i, half)[...] + (recv[one] + recv[two])
        for copy in copies:
            copy.wait_send()

    def part1_0(shard, half):
        return core0.at[2 * shard + half]

    def part1_1(shard, half):
        return core1.at[
            pl.ds(4 * (shard // 2) + 2 * half, 2), rows8(lax.rem(shard, 2) * HALF, HALF)
        ]

    def part2_0(shard, half):
        return core0.at[
            2 * z + shard // 2, rows8(lax.rem(shard, 2) * HALF + half * QUART, QUART)
        ]

    def part2_1(shard, half):
        return core1.at[4 * (y // 2) + shard, rows8(lax.rem(y, 2) * HALF + half * QUART, QUART)]

    swap0.wait_recv()
    core_add(0)
    ring0 = ring_start(0, z, z_next, z_prev, part1_0, rs1_0)
    swap1.wait_recv()
    core_add(1)
    ring1 = ring_start(1, y, y_next, y_prev, part1_1, rs1_1)

    grad_input[...] = conv(2, 0, True).reshape(T, H, W, C)

    ring_middle(0, z, z_next, z_prev, part1_0, rs1_0, ring0)
    ring_middle(1, y, y_next, y_prev, part1_1, rs1_1, ring1)
    ring_end(z, part1_0, rs1_0, ring0, [part1_0(z, 0), part1_0(z, 1)])
    ring2 = ring_start(2, y, y_next, y_prev, part2_0, rs2_0)
    ring_end(y, part1_1, rs1_1, ring1, [part1_1(y, 0), part1_1(y, 1)])
    ring3 = ring_start(3, z, z_next, z_prev, part2_1, rs2_1)
    ring_middle(2, y, y_next, y_prev, part2_0, rs2_0, ring2)
    ring_middle(3, z, z_next, z_prev, part2_1, rs2_1, ring3)

    def tot_halves(f):
        return [tot.at[f, pl.ds(0, QUART)], tot.at[f, pl.ds(QUART, QUART)]]

    across = ((flip2, other, wa), (ta, other, wa))
    x_copies = []

    def x_start(step, f, src):
        copy = remote(
            src.at[f], x_recv.at[step, f], x_send.at[step, f], x_rcv.at[step, f], across[step]
        )
        copy.start()
        x_copies.append(copy)
        return copy

    ring_end(y, part2_0, rs2_0, ring2, tot_halves(0))
    first_x = [x_start(0, 0, tot)]
    ring_end(z, part2_1, rs2_1, ring3, tot_halves(1))
    first_x.append(x_start(0, 1, tot))
    second_x = []
    for f in range(2):
        first_x[f].wait_recv()
        tot2[f] = tot[f] + x_recv[0, f]
        second_x.append(x_start(1, f, tot2))
    for f in range(2):
        second_x[f].wait_recv()
        tot3[f] = tot2[f] + x_recv[1, f]

    holder = y // 2 == x_hi
    mine = lax.rem(y, 2)

    def shares():
        return [
            remote(
                tot3, full.at[mine], ag_send.at[step - 1], ag_recv.at[mine],
                (ta, ha, mod(wa + step, 4)),
            )
            for step in (1, 2, 3)
        ]

    @pl.when(holder)
    def _():
        for copy in shares():
            copy.start()
        full[mine] = tot3[...]

    for part in range(2):

        @pl.when(y != 2 * x_hi + part)
        def _(part=part):
            remote(
                tot3, full.at[part], ag_send.at[0], ag_recv.at[part], (ta, ha, mod(wa + 1, 4))
            ).wait_recv()

    squares = jnp.zeros((8, C), f32)
    for f in range(2):
        low, high = full[0, f], full[1, f, : OWN - HALF]
        squares += jnp.sum((low * low).reshape(-1, 8, C), axis=0)
        squares += jnp.sum((high * high).reshape(-1, 8, C), axis=0)
    note[:8] = squares
    note[8:] = full[1, 1, OWN - HALF :]
    notes[ta] = note[...]

    def tell(step):
        return remote(
            note, notes.at[ta], n_send.at[step], n_recv.at[ta], (mod(ta + step, 16), ha, wa)
        )

    def heard(step):
        source = mod(ta - step, 16)
        return remote(
            note, notes.at[source], n_send.at[step], n_recv.at[source], (source, ha, wa)
        )

    for step in range(1, 16):
        tell(step).start()
    for step in range(1, 16):
        heard(step).wait_recv()
    everything = jnp.sum(notes[:, :8], axis=0)
    raw_bias = jnp.sum(notes[0, 8:], axis=0, keepdims=True)
    norm2 = jnp.sum(everything, axis=(0, 1), keepdims=True) + jnp.sum(
        raw_bias * raw_bias, axis=(0, 1), keepdims=True
    )
    factor = jnp.minimum(1.0, jnp.sqrt(jnp.full((1, 1), LIMIT, f32)) / jnp.sqrt(norm2))
    for f, out in ((0, grad_second), (1, grad_first)):
        out[:HALF] = full[0, f] * factor
        out[HALF:] = full[1, f, : OWN - HALF] * factor
    grad_bias[...] = raw_bias * factor

    for copies in plain + strips:
        for copy in copies:
            copy.wait_send()
    swap0.wait_send()
    swap1.wait_send()
    for copy in x_copies:
        copy.wait_send()

    @pl.when(holder)
    def _():
        for copy in shares():
            copy.wait_send()

    for step in range(1, 16):
        tell(step).wait_send()


def per_device(video_in, first_filter, first_bias, second_filter, grad_output):
    vmem = pltpu.VMEM
    dma = pltpu.SemaphoreType.DMA
    any_spec = pl.BlockSpec(memory_space=pl.ANY)
    vmem_spec = pl.BlockSpec(memory_space=pltpu.VMEM)
    outs = pl.pallas_call(
        kernel,
        out_shape=(
            jax.ShapeDtypeStruct((T, H, W, C), f32),
            jax.ShapeDtypeStruct((OWN, C), f32),
            jax.ShapeDtypeStruct((OWN, C), f32),
            jax.ShapeDtypeStruct((1, C), f32),
        ),
        in_specs=[any_spec, any_spec, vmem_spec, any_spec, any_spec],
        out_specs=[vmem_spec] * 4,
        scratch_shapes=[
            vmem((2, 27, C, C), f32),
            vmem((2, 27, C, 2 * C), bf16),
            vmem((3, T + 2, H + 2, 32, C), f32),
            vmem((3, 2, T, H, 1, C), f32),
            vmem((3, 2, T + 2, H + 2, 1, C), f32),
            vmem((3, 3, T + 2, H + 2, W, 2 * C), bf16),
            vmem((V, 2 * C), f32),
            vmem((V, C), f32),
            vmem((2 * C, V), bf16),
            vmem((2 * C, V), bf16),
            vmem((2, ROWS, C), f32),
            vmem((8, C), f32),
            vmem((2, 8, PAD, C), f32),
            vmem((8, PAD, C), f32),
            vmem((8, PAD, C), f32),
            vmem((6, PAD, C), f32),
            vmem((6, 2, HALF, C), f32),
            vmem((6, QUART, C), f32),
            vmem((6, QUART, C), f32),
            vmem((2, HALF, C), f32),
            vmem((2, 2, HALF, C), f32),
            vmem((2, HALF, C), f32),
            vmem((2, HALF, C), f32),
            vmem((2, 2, HALF, C), f32),
            vmem((16, C), f32),
            vmem((16, 16, C), f32),
            dma((4,)),
            dma((3, 11)),
            dma((3, 11)),
            dma((2,)),
            dma((2,)),
            dma((4, 6)),
            dma((4, 6)),
            dma((2, 2)),
            dma((2, 2)),
            dma((3,)),
            dma((2,)),
            dma((16,)),
            dma((16,)),
        ],
        compiler_params=pltpu.CompilerParams(
            collective_id=0, has_side_effects=True, vmem_limit_bytes=56 * 1024 * 1024
        ),
        cost_estimate=pl.CostEstimate(
            flops=5 * 2 * V * ROWS * C, bytes_accessed=6 * 2**20, transcendentals=2 * V * C
        ),
    )(video_in, first_filter, first_bias.reshape(1, C), second_filter, grad_output)
    grad_input, grad_first, grad_second, grad_bias = outs
    return grad_input, grad_first, grad_second, grad_bias.reshape(C)


def solution(mesh):
    placed = (P("ta", "ha", "wa", None), P(), P(), P(), P("ta", "ha", "wa", None))
    return jax.shard_map(
        per_device,
        mesh=mesh,
        in_specs=placed,
        out_specs=(P("ta", "ha", "wa", None), P("ta", None), P("ta", None), P()),
        check_vma=False,
    )
```

time: 410 us -> 83 us (0.20); the launches traced: 405 us -> 82.8 us
  waiting for transfers between devices: 163 us -> 0 us
  Pallas kernels: 0 us -> 76.2 us
  matrix products: 59 us -> 0 us
  starting transfers between devices: 55.9 us -> 0 us
  blocking collectives: 52.8 us -> 0 us
  local copies, waits for them, and re-layouts: 42.9 us -> 5.92 us
  between operations: 18.3 us -> 0.64 us
  other arithmetic: 12.7 us -> 0 us
    unnamed x5 -> x0, waiting for transfers between devices: 93.8 us -> none
    pallas_call x0 -> x1, Pallas kernels: none -> 76.2 us  [per_device(): pl.pallas_call(kernel, out_shape=(jax.ShapeDtypeStruct((T, H, W, C), f32)...]
    psum x1 -> x0, waiting for transfers between devices: 66.8 us -> none  [per_device(): lax.psum((raw_first, raw_second, raw_bias), ('ha', 'wa'))]
    dot_general x15 -> x0, matrix products: 59 us -> none  [the longest x6 23.6 us: weight_taps(): lax.dot_general(columns, flat_cot, (((0,), (0,)), ((), ())), precision=HI...]
    ppermute x20 -> x0, starting transfers between devices: 55.6 us -> none  [the longest x8 30.4 us: extended_2(): lax.ppermute(lax.slice_in_dim(block, block.shape[dim] - width, None, axis...]
    psum x2 -> x0, blocking collectives: 52.8 us -> none  [the longest x1 38.6 us: per_device(): filter_squares, bias_total = lax.psum((share_squares, plane_bias), 'ta')]
    unnamed x188 -> x4, local copies, waits for them, and re-layouts: 21.7 us -> 5.92 us
    transpose x4 -> x0, local copies, waits for them, and re-layouts: 9.75 us -> none  [transpose_taps(): jnp.transpose(filters[9 * tap_t:9 * tap_t + 9], (0, 2, 1))]
  transfers between devices with their start and end apart: 23 -> 0, of which waited for: 4 -> 0; matrix products, arithmetic and copies ran while one was open for 18% -> 0% of each run, Pallas kernels for 0% -> 0%
where the time goes in v1:
time: 83 us; the launch traced here: 82.8 us
  Pallas kernels  76.2 us (92%)
  local copies, waits for them, and re-layouts  5.92 us (7%)
    pallas_call x1, Pallas kernels, per_device(): pl.pallas_call(kernel, out_shape=(jax.ShapeDtypeStruct((T, H, W, C), f32)...  76.2 us
    unnamed x4, local copies, waits for them, and re-layouts  5.92 us

profile of v1, /device:TPU:1, one launch (start us, length us, event | category | flops | bytes accessed | tf_op | source)
XLA Modules:
  0.0 82.8 jit_solution(14822018029440145772)
XLA Ops:
  0.6 76.2 %shard_map.84 = (f32[4,8,16,128]{3,2,1,0:T(8,128)}, f32[216,128]{1,0:T(8,128)}, f32[216,128]{1,0:T(8,128)}, f32[1,128]{1,0:T(1,128)}) custom-call(f32[4,8,16,128]{3,2,1,0:T(8,128)} %video.1, f32[27,128,128]{2,1,0:T(8,128)} %first.1, f32[1,128]{1,0:T(1,128)} %bitcast.2, f32[27,128,128]{2,1,0:T(8,128)} %second.1, f32[4,8,16,128]{3,2,1,0:T(8,128)} %cot.1), custom_call_target="tpu_custom_call" | custom-call | flops 2264924160 | bytes 6291456 | tf_op jit(solution)/shard_map/pallas_call | solution.py:490
  76.8 1.7 %copy.13 = f32[4,8,16,128]{3,2,1,0:T(8,128)} copy(f32[4,8,16,128]{3,2,1,0:T(8,128)} %get-tuple-element.16) | data formatting | bytes 524288
  78.5 1.5 %copy.14 = f32[216,128]{1,0:T(8,128)} copy(f32[216,128]{1,0:T(8,128)} %get-tuple-element.17) | data formatting | bytes 221184
  80.1 1.5 %copy.15 = f32[216,128]{1,0:T(8,128)} copy(f32[216,128]{1,0:T(8,128)} %get-tuple-element.18) | data formatting | bytes 221184
  81.6 1.1 %copy.16 = f32[128]{0:T(128)} copy(f32[128]{0:T(128)} %bitcast.3) | data formatting | bytes 1024

commit v2 on v1

v2 whole, which is shorter than its diff:
```python
import jax
import jax.numpy as jnp
from jax import lax
from jax.experimental import pallas as pl
from jax.experimental.pallas import tpu as pltpu
from jax.sharding import PartitionSpec as P

f32, bf16 = jnp.float32, jnp.bfloat16
MESH = pl.DeviceIdType.MESH
C = 128
T, H, W = 4, 8, 16
V = T * H * W
ROWS = 27 * C
OWN = ROWS // 16
PAD = OWN + 8
HALF = PAD // 2
QUART = HALF // 2
LEFT = 8
LIMIT = float(54 * C * C + C)


def split(value):
    high = value.astype(bf16)
    low = (value - high.astype(f32)).astype(bf16)
    return high, low


def mod(value, count):
    return lax.rem(value + 2 * count, count)


def rows8(start, size):
    return pl.ds(pl.multiple_of(start, 8), size)


def remote(src, dst, send, recv, device):
    return pltpu.make_async_remote_copy(
        src_ref=src, dst_ref=dst, send_sem=send, recv_sem=recv, device_id=device,
        device_id_type=MESH,
    )


def kernel(
    video, first, bias, second, cot,
    grad_input, grad_first, grad_second, grad_bias,
    w_f32, w_split, ext, cols, cols_ext, shifted, acc, pre_ref, act_t, grad_t,
    raw, bias8, pack, summed, line_recv, line, plane_recv, share, full,
    note, notes, note2, notes2,
    local_sem, halo_send, halo_recv, core_send, core_recv, line_send, line_rcv,
    plane_send, plane_rcv, ag_send, ag_recv, n_send, n_recv, n2_send, n2_recv,
):
    ta, ha, wa = lax.axis_index("ta"), lax.axis_index("ha"), lax.axis_index("wa")
    core = lax.rem(ta, 2)
    x_hi = lax.rem(ta // 2, 2)
    z = ta // 4
    y = wa
    other = 1 - ha

    own_at = (2, 0, 0)
    blocks = [
        pltpu.make_async_copy(
            src, ext.at[n, pl.ds(own_at[n], T), pl.ds(1, H), pl.ds(LEFT, W)], local_sem.at[n]
        )
        for n, src in enumerate((video, cot))
    ]
    loads = [
        pltpu.make_async_copy(src, w_f32.at[n], local_sem.at[2 + n])
        for n, src in enumerate((first, second))
    ]
    for copy in blocks + loads:
        copy.start()

    gap = 9 * ha
    for n in range(3):
        ext[n, :, pl.ds(gap, 1)] = jnp.zeros((T + 2, 1, 32, C), f32)
        cols_ext[n, :, :, pl.ds(gap, 1)] = jnp.zeros((2, T + 2, 1, 1, C), f32)

    barrier = pltpu.get_barrier_semaphore()
    x = 2 * x_hi + ha

    def place(px, py, pz, pc):
        return (4 * pz + 2 * (px // 2) + pc, lax.rem(px, 2), py)

    xs = [mod(x + step, 4) for step in range(4)]
    ys = [mod(y + step, 4) for step in range(4)]
    zs = [mod(z + step, 4) for step in range(4)]
    plane_xy = [(i, j) for i in range(4) for j in range(4) if i or j]
    greeted = [place(xs[i], ys[j], z, core) for i, j in plane_xy]
    greeted += [place(xs[i], y, zs[j], core) for i in range(4) for j in (1, 2, 3)]
    greeted += [place(x, y, zs[j], 1 - core) for j in range(4)]
    greeted.append((mod(ta + 2 * core - 1, 16), ha, wa))
    for dt in (-1, 1):
        for row in (ha, other):
            for dw in (-1, 0, 1):
                if not (row is ha and dw == 0):
                    greeted.append((mod(ta + dt, 16), row, mod(wa + dw, 4)))
    for device in greeted:
        pl.semaphore_signal(barrier, inc=1, device_id=device, device_id_type=MESH)

    halo_at = (0, 4, 4)
    edge_at = (2, 0, 0)
    along = (1, -1, -1)
    edge_row = 7 * other

    def halo_plain(n, src):
        copies = []
        for slot, (dt, dh) in enumerate(((0, 1), (1, 0), (1, 1))):
            frames = pl.ds(edge_at[n], 2) if dt else pl.ds(0, T)
            to = pl.ds(halo_at[n], 2) if dt else pl.ds(own_at[n], T)
            rows = pl.ds(edge_row, 1) if dh else pl.ds(0, H)
            to_rows = pl.ds(gap, 1) if dh else pl.ds(1, H)
            copies.append(
                remote(
                    src(frames, rows),
                    ext.at[n, to, to_rows, pl.ds(LEFT, W)],
                    halo_send.at[n, slot], halo_recv.at[n, slot],
                    (mod(ta + along[n] * dt, 16), other if dh else ha, wa),
                )
            )
        return copies

    def halo_columns(n):
        copies = []
        slot = 3
        for dt in (0, 1):
            for dh in (0, 1):
                for side, dw in ((0, -1), (1, 1)):
                    if dt + dh + abs(dw) == 0:
                        continue
                    frames = pl.ds(edge_at[n], 2) if dt else pl.ds(0, T)
                    to = pl.ds(halo_at[n], 2) if dt else pl.ds(own_at[n], T)
                    rows = pl.ds(edge_row, 1) if dh else pl.ds(0, H)
                    to_rows = pl.ds(gap, 1) if dh else pl.ds(1, H)
                    copies.append(
                        remote(
                            cols.at[n, side, frames, rows],
                            cols_ext.at[n, 1 - side, to, to_rows],
                            halo_send.at[n, slot], halo_recv.at[n, slot],
                            (mod(ta + along[n] * dt, 16), other if dh else ha, mod(wa + dw, 4)),
                        )
                    )
                    slot += 1
        return copies

    def pack_columns(n):
        own = ext[n, pl.ds(own_at[n], T), pl.ds(1, H), pl.ds(LEFT, W)]
        cols[n, 0] = own[:, :, 0:1]
        cols[n, 1] = own[:, :, W - 1 : W]

    plain = [halo_plain(0, lambda t, h: video.at[t, h]), halo_plain(1, lambda t, h: cot.at[t, h])]
    strips = [halo_columns(0), halo_columns(1)]
    for n in (0, 1):
        blocks[n].wait()
        pack_columns(n)

    for copy in loads:
        copy.wait()

    def split_filters(tap, _):
        for n in range(2):
            high, low = split(w_f32[n, tap])
            w_split[n, tap, :, :C] = high
            w_split[n, tap, :, C:] = low
        return 0

    lax.fori_loop(0, 27, split_filters, 0)

    pl.semaphore_wait(barrier, len(greeted))
    for n in (0, 1):
        for copy in plain[n] + strips[n]:
            copy.start()

    def transposed(value, ref):
        high, low = split(value.T)
        ref[:C] = high
        ref[C:] = low

    left_in = (wa > 0).astype(f32)
    right_in = (wa < 3).astype(f32)
    frame_in = ((ta > 0).astype(f32), (ta < 15).astype(f32), (ta < 15).astype(f32))

    def shift_columns(n):
        def frame(t, _):
            ext[n, t, :, LEFT - 1 : LEFT] = cols_ext[n, 0, t] * left_in
            ext[n, t, :, LEFT + W : LEFT + W + 1] = cols_ext[n, 1, t] * right_in
            is_halo = jnp.logical_and(t >= halo_at[n], t < halo_at[n] + 2)
            keep = jnp.where(is_halo, frame_in[n], 1.0)
            for c in range(3):
                high, low = split(ext[n, t, :, LEFT - 1 + c : LEFT - 1 + c + W] * keep)
                shifted[n, c, t, :, :, :C] = high
                shifted[n, c, t, :, :, C:] = low
            return 0

        lax.fori_loop(0, T + 2, frame, 0)

    def conv(n, filters, back):
        for a in range(3):
            pieces, blocks_w = [], []
            for b in range(3):
                for c in range(3):
                    at = (2 - a, 2 - b, 2 - c) if back else (a, b, c)
                    window = shifted[n, at[2], pl.ds(at[0], T), pl.ds(at[1], H)]
                    pieces.append(window.reshape(V, 2 * C))
                    w = w_split[filters, 9 * a + 3 * b + c]
                    if back:
                        high, low = w[:, :C], w[:, C:]
                        blocks_w.append(
                            jnp.concatenate(
                                [
                                    jnp.concatenate([high, high], axis=1),
                                    jnp.concatenate([low, low], axis=1),
                                ],
                                axis=0,
                            )
                        )
                    else:
                        blocks_w += [w, w]
            columns = jnp.concatenate(pieces, axis=1)
            if back:
                product = lax.dot_general(
                    columns, jnp.concatenate(blocks_w, axis=1), (((1,), (1,)), ((), ())),
                    preferred_element_type=f32,
                )
            else:
                product = jnp.dot(
                    columns, jnp.concatenate(blocks_w, axis=0), preferred_element_type=f32
                )
            if a == 0:
                acc[...] = product
            else:
                acc[...] += product
        return acc[:, :C] + acc[:, C:]

    def weight_grad(fixed, n, f):
        def taps(step, _):
            p, q = step // 3, lax.rem(step, 3)
            for c in range(3):
                at = (p, q, c) if f else (2 - p, 2 - q, 2 - c)
                window = shifted[n, at[2], pl.ds(at[0], T), pl.ds(at[1], H)].reshape(V, 2 * C)
                o = jnp.dot(fixed[...], window, preferred_element_type=f32)
                o = (o[:C, :C] + o[C:, :C]) + (o[:C, C:] + o[C:, C:])
                raw[f, rows8((3 * step + c) * C, C)] = o.T if f else o
            return 0

        lax.fori_loop(0, 9, taps, 0)

    pieces = ((0, HALF), (HALF, QUART), (HALF + QUART, QUART - 8))

    def slots(kz, kx):
        return (
            (0, kz, kx * HALF),
            (1, 2 * kx, kz * QUART),
            (1, 2 * kx + 1, kz * QUART),
        )

    owners = [(kz, kx) for kz in range(4) for kx in range(2)]

    def core_swap(f):
        for kz, kx in owners:
            k = 4 * kz + 2 * kx + 1 - core
            for (start, size), (part, shard, to) in zip(pieces, slots(kz, kx)):
                pack[f, part, shard, to : to + size] = raw[f, rows8(OWN * k + start, size)]
            tail = kz * QUART + QUART - 8
            pack[f, 1, 2 * kx + 1, tail : tail + 8] = bias8[...] if f else jnp.zeros((8, C), f32)
        copy = remote(
            pack.at[f], summed.at[f], core_send.at[f], core_recv.at[f],
            (ta + 1 - 2 * core, ha, wa),
        )
        copy.start()
        return copy

    def core_add(f):
        for kz, kx in owners:
            k = 4 * kz + 2 * kx + core
            for (start, size), (part, shard, to) in zip(pieces, slots(kz, kx)):
                summed[f, part, shard, to : to + size] += raw[f, rows8(OWN * k + start, size)]
            if f:
                tail = kz * QUART + QUART - 8
                summed[f, 1, 2 * kx + 1, tail : tail + 8] += bias8[...]

    def line_start(f):
        copies = []
        for step in (1, 2, 3):
            for part, shard, device in (
                (0, zs[step], place(x, y, zs[step], core)),
                (1, ys[step], place(x, ys[step], z, core)),
            ):
                copies.append(
                    remote(
                        summed.at[f, part, shard], line_recv.at[f, part, step - 1],
                        line_send.at[f, part, step - 1], line_rcv.at[f, part, step - 1], device,
                    )
                )
        for copy in copies:
            copy.start()
        return copies

    def line_end(f, copies):
        for copy in copies:
            copy.wait_recv()
        for part, own in ((0, z), (1, y)):
            line[f, part] = (summed[f, part, own] + line_recv[f, part, 0]) + (
                line_recv[f, part, 1] + line_recv[f, part, 2]
            )

    def piece(part, px, other_axis):
        if part == 0:
            slot = 4 * lax.rem(other_axis, 2) + px
            return (other_axis // 2) * HALF + 16 * jnp.minimum(slot, 6)
        return other_axis * QUART + jnp.minimum(16 * px, 40)

    across = (y, z)

    def plane_copies(f):
        copies = []
        for part in (0, 1):
            mine = 4 * x + across[part]
            for n, (i, j) in enumerate(plane_xy):
                to = (ys, zs)[part][j]
                device = place(xs[i], to, z, core) if part == 0 else place(xs[i], y, to, core)
                copies.append(
                    remote(
                        line.at[f, part, rows8(piece(part, xs[i], to), 16)],
                        plane_recv.at[f, part, mine],
                        plane_send.at[f, part, n], plane_rcv.at[f, part, mine], device,
                    )
                )
        return copies

    def plane_start(f):
        copies = plane_copies(f)
        for copy in copies:
            copy.start()
        for part in (0, 1):
            plane_recv[f, part, 4 * x + across[part]] = line[
                f, part, rows8(piece(part, x, across[part]), 16)
            ]
        return copies

    def plane_end(f):
        for part in (0, 1):
            for n, (i, j) in enumerate(plane_xy):
                source = (ys, zs)[part][j]
                slot = 4 * xs[i] + source
                device = (
                    place(xs[i], source, z, core) if part == 0 else place(xs[i], y, source, core)
                )
                remote(
                    line.at[f, part, pl.ds(0, 16)], plane_recv.at[f, part, slot],
                    plane_send.at[f, part, n], plane_rcv.at[f, part, slot], device,
                ).wait_recv()
            share[f, part] = jnp.sum(plane_recv[f, part], axis=0)

    for copy in plain[0] + strips[0]:
        copy.wait_recv()
    shift_columns(0)
    pre = conv(0, 0, False) + bias[...]
    pre_ref[...] = pre
    sig = 1.0 / (1.0 + jnp.exp(-pre))
    transposed(pre * sig, act_t)

    for copy in plain[1] + strips[1]:
        copy.wait_recv()
    shift_columns(1)
    weight_grad(act_t, 1, 0)
    swap0 = core_swap(0)

    grad_act = conv(1, 1, True)
    pre = pre_ref[...]
    sig = 1.0 / (1.0 + jnp.exp(-pre))
    grad_pre = grad_act * sig * (1.0 + pre * (1.0 - sig))
    bias8[...] = jnp.sum(grad_pre.reshape(V // 8, 8, C), axis=0)
    ext[2, pl.ds(0, T), pl.ds(1, H), pl.ds(LEFT, W)] = grad_pre.reshape(T, H, W, C)
    transposed(grad_pre, grad_t)

    swap0.wait_recv()
    core_add(0)
    line0 = line_start(0)

    plain.append(
        halo_plain(2, lambda t, h: ext.at[2, t, pl.ds(h.start + 1, h.size), pl.ds(LEFT, W)])
    )
    pack_columns(2)
    strips.append(halo_columns(2))
    for copy in plain[2] + strips[2]:
        copy.start()

    weight_grad(grad_t, 0, 1)
    swap1 = core_swap(1)
    swap1.wait_recv()
    core_add(1)
    line1 = line_start(1)

    line_end(0, line0)
    plane0 = plane_start(0)

    for copy in plain[2] + strips[2]:
        copy.wait_recv()
    shift_columns(2)
    grad_input[...] = conv(2, 0, True).reshape(T, H, W, C)

    line_end(1, line1)
    plane1 = plane_start(1)
    plane_end(0)
    plane_end(1)

    last = x == 3
    odd = lax.rem(y, 2) == 1
    keep_low = jnp.where(jnp.logical_and(last, odd), 0.0, 1.0)
    keep_first = jnp.where(last, 0.0, 1.0)
    squares = jnp.zeros((8, C), f32)
    for f in range(2):
        squares += keep_low * (
            share[f, 0, :8] * share[f, 0, :8] + share[f, 0, 8:] * share[f, 0, 8:]
        )
        squares += keep_first * (share[f, 1, :8] * share[f, 1, :8])
        squares += keep_low * (share[f, 1, 8:] * share[f, 1, 8:])
    note[:8] = squares
    note[8:] = share[1, 1, 8:]
    here = 4 * x + y
    notes[here] = note[...]

    def tell(n, i, j, slot):
        return remote(
            note, notes.at[slot], n_send.at[n], n_recv.at[slot], place(xs[i], ys[j], z, core)
        )

    for n, (i, j) in enumerate(plane_xy):
        tell(n, i, j, here).start()

    wide = y // 2
    half_slot = 4 * lax.rem(y, 2) + x

    def give(i, j):
        return remote(
            share, full.at[half_slot], ag_send.at[4 * i + j], ag_recv.at[half_slot],
            place(2 * wide + i, ys[j], z, core),
        )

    def each_give(act_on):
        for i in range(2):

            @pl.when(2 * wide + i != x)
            def _(i=i):
                act_on(give(i, 0))

            for j in (1, 2, 3):
                act_on(give(i, j))

    each_give(lambda copy: copy.start())

    @pl.when(wide == x_hi)
    def _():
        full[half_slot] = share[...]

    for n, (i, j) in enumerate(plane_xy):
        tell(n, i, j, 4 * xs[i] + ys[j]).wait_recv()
    note2[:8] = jnp.sum(notes[:, :8], axis=0)
    note2[8:] = notes[13, 8:]
    there = 2 * z + core
    notes2[there] = note2[...]
    line_zc = [(j, c) for j in range(4) for c in range(2) if j or c]

    def tell2(n, j, c, slot):
        to_core = 1 - core if c else core
        return remote(
            note2, notes2.at[slot], n2_send.at[n], n2_recv.at[slot], place(x, y, zs[j], to_core)
        )

    for n, (j, c) in enumerate(line_zc):
        tell2(n, j, c, there).start()

    for part in range(2):
        for i in range(4):

            @pl.when(jnp.logical_or(x != i, y != 2 * x_hi + part))
            def _(part=part, i=i):
                slot = 4 * part + i
                remote(
                    share, full.at[slot], ag_send.at[0], ag_recv.at[slot],
                    place(x, ys[1], z, core),
                ).wait_recv()

    for n, (j, c) in enumerate(line_zc):
        tell2(n, j, c, 2 * zs[j] + (1 - core if c else core)).wait_recv()
    everything = jnp.sum(notes2[:, :8], axis=0)
    raw_bias = jnp.sum(notes2[0, 8:], axis=0, keepdims=True)
    norm2 = jnp.sum(everything, axis=(0, 1), keepdims=True) + jnp.sum(
        raw_bias * raw_bias, axis=(0, 1), keepdims=True
    )
    factor = jnp.minimum(1.0, jnp.sqrt(jnp.full((1, 1), LIMIT, f32)) / jnp.sqrt(norm2))
    for f, out in ((0, grad_second), (1, grad_first)):
        for slot in range(8):
            low = 16 * min(slot, 6)
            out[low : low + 16] = full[slot, f, 0] * factor
            high = HALF + QUART * (slot // 4) + min(16 * (slot % 4), 40)
            size = min(16, OWN - high)
            out[high : high + size] = full[slot, f, 1, :size] * factor
    grad_bias[...] = raw_bias * factor

    for copies in plain + strips + [[swap0, swap1], line0, line1, plane0, plane1]:
        for copy in copies:
            copy.wait_send()
    for n, (i, j) in enumerate(plane_xy):
        tell(n, i, j, here).wait_send()
    each_give(lambda copy: copy.wait_send())
    for n, (j, c) in enumerate(line_zc):
        tell2(n, j, c, there).wait_send()


def hand_over(*refs):
    for source, out in zip(refs[:4], refs[4:]):
        out[...] = source[...]


def per_device(video_in, first_filter, first_bias, second_filter, grad_output):
    vmem = pltpu.VMEM
    dma = pltpu.SemaphoreType.DMA
    any_spec = pl.BlockSpec(memory_space=pl.ANY)
    vmem_spec = pl.BlockSpec(memory_space=pltpu.VMEM)
    shapes = (
        jax.ShapeDtypeStruct((T, H, W, C), f32),
        jax.ShapeDtypeStruct((OWN, C), f32),
        jax.ShapeDtypeStruct((OWN, C), f32),
        jax.ShapeDtypeStruct((1, C), f32),
    )
    outs = pl.pallas_call(
        kernel,
        out_shape=shapes,
        in_specs=[any_spec, any_spec, vmem_spec, any_spec, any_spec],
        out_specs=[vmem_spec] * 4,
        scratch_shapes=[
            vmem((2, 27, C, C), f32),
            vmem((2, 27, C, 2 * C), bf16),
            vmem((3, T + 2, H + 2, 32, C), f32),
            vmem((3, 2, T, H, 1, C), f32),
            vmem((3, 2, T + 2, H + 2, 1, C), f32),
            vmem((3, 3, T + 2, H + 2, W, 2 * C), bf16),
            vmem((V, 2 * C), f32),
            vmem((V, C), f32),
            vmem((2 * C, V), bf16),
            vmem((2 * C, V), bf16),
            vmem((2, ROWS, C), f32),
            vmem((8, C), f32),
            vmem((2, 2, 4, PAD, C), f32),
            vmem((2, 2, 4, PAD, C), f32),
            vmem((2, 2, 3, PAD, C), f32),
            vmem((2, 2, PAD, C), f32),
            vmem((2, 2, 16, 16, C), f32),
            vmem((2, 2, 16, C), f32),
            vmem((8, 2, 2, 16, C), f32),
            vmem((16, C), f32),
            vmem((16, 16, C), f32),
            vmem((16, C), f32),
            vmem((8, 16, C), f32),
            dma((4,)),
            dma((3, 11)),
            dma((3, 11)),
            dma((2,)),
            dma((2,)),
            dma((2, 2, 3)),
            dma((2, 2, 3)),
            dma((2, 2, 15)),
            dma((2, 2, 16)),
            dma((8,)),
            dma((8,)),
            dma((15,)),
            dma((16,)),
            dma((7,)),
            dma((8,)),
        ],
        compiler_params=pltpu.CompilerParams(
            collective_id=0, has_side_effects=True, vmem_limit_bytes=56 * 1024 * 1024
        ),
        cost_estimate=pl.CostEstimate(
            flops=5 * 2 * V * ROWS * C, bytes_accessed=6 * 2**20, transcendentals=2 * V * C
        ),
    )(video_in, first_filter, first_bias.reshape(1, C), second_filter, grad_output)
    outs = pl.pallas_call(
        hand_over, out_shape=shapes, in_specs=[vmem_spec] * 4, out_specs=[vmem_spec] * 4
    )(*outs)
    grad_input, grad_first, grad_second, grad_bias = outs
    return grad_input, grad_first, grad_second, grad_bias.reshape(C)


def solution(mesh):
    placed = (P("ta", "ha", "wa", None), P(), P(), P(), P("ta", "ha", "wa", None))
    return jax.shard_map(
        per_device,
        mesh=mesh,
        in_specs=placed,
        out_specs=(P("ta", "ha", "wa", None), P("ta", None), P("ta", None), P()),
        check_vma=False,
    )
```

time: 83 us -> 63.5 us (0.77)
  Pallas kernels: 76.2 us -> 62.7 us
  local copies, waits for them, and re-layouts: 5.92 us -> 0 us
    pallas_call x1 -> x2, Pallas kernels: 76.2 us -> 62.7 us  [the longest x1 60.9 us: per_device(): pl.pallas_call(kernel, out_shape=shapes, in_specs=[any_spec, any_spec, vm...]
    unnamed x4 -> x0, local copies, waits for them, and re-layouts: 5.92 us -> none
where the time goes in v2:
time: 63.5 us; the launch traced here: 63.4 us
  Pallas kernels  62.7 us (99%)
  between operations  0.64 us (1%)
    pallas_call x1, Pallas kernels, per_device(): pl.pallas_call(kernel, out_shape=shapes, in_specs=[any_spec, any_spec, vm...  60.9 us
    pallas_call x1, Pallas kernels, per_device(): pl.pallas_call(hand_over, out_shape=shapes, in_specs=[vmem_spec] * 4, out...  1.81 us

profile of v2, /device:TPU:1, one launch (start us, length us, event | category | flops | bytes accessed | tf_op | source)
XLA Modules:
  0.0 63.4 jit_solution(4212464577633263790)
XLA Ops:
  0.6 60.9 %shard_map.84 = (f32[4,8,16,128]{3,2,1,0:T(8,128)}, f32[216,128]{1,0:T(8,128)}, f32[216,128]{1,0:T(8,128)}, f32[1,128]{1,0:T(1,128)}) custom-call(f32[4,8,16,128]{3,2,1,0:T(8,128)} %video.1, f32[27,128,128]{2,1,0:T(8,128)} %first.1, f32[1,128]{1,0:T(1,128)} %bitcast.2, f32[27,128,128]{2,1,0:T(8,128)} %second.1, f32[4,8,16,128]{3,2,1,0:T(8,128)} %cot.1), custom_call_target="tpu_custom_call" | custom-call | flops 2264924160 | bytes 6291456 | tf_op jit(solution)/shard_map/pallas_call | solution.py:527
  61.6 1.8 %shard_map.85 = (f32[4,8,16,128]{3,2,1,0:T(8,128)}, f32[216,128]{1,0:T(8,128)}, f32[216,128]{1,0:T(8,128)}, f32[1,128]{1,0:T(1,128)}) custom-call(f32[4,8,16,128]{3,2,1,0:T(8,128)} %get-tuple-element.12.refs_0_, f32[216,128]{1,0:T(8,128)} %get-tuple-element.13.refs_1_, f32[216,128]{1,0:T(8,128)} %get-tuple-element.14.refs_2_, f32[1,128]{1,0:T(1,128)} %get-tuple-element.15.refs_3_), custom_call_target="tpu_custom_call" | custom-call | tf_op jit(solution)/shard_map/pallas_call | solution.py:579

commit v3 on v2

--- a/solution.py
+++ b/solution.py
@@ -47,7 +47,7 @@
     raw, bias8, pack, summed, line_recv, line, plane_recv, share, full,
     note, notes, note2, notes2,
     local_sem, halo_send, halo_recv, core_send, core_recv, line_send, line_rcv,
-    plane_send, plane_rcv, ag_send, ag_recv, n_send, n_recv, n2_send, n2_recv,
+    plane_send, plane_rcv, ag_send, ag_recv, n_send, n_recv,
 ):
     ta, ha, wa = lax.axis_index("ta"), lax.axis_index("ha"), lax.axis_index("wa")
     core = lax.rem(ta, 2)
@@ -84,16 +84,21 @@
     xs = [mod(x + step, 4) for step in range(4)]
     ys = [mod(y + step, 4) for step in range(4)]
     zs = [mod(z + step, 4) for step in range(4)]
+    hops = (0, 1, 2, 1)
     plane_xy = [(i, j) for i in range(4) for j in range(4) if i or j]
-    greeted = [place(xs[i], ys[j], z, core) for i, j in plane_xy]
-    greeted += [place(xs[i], y, zs[j], core) for i in range(4) for j in (1, 2, 3)]
-    greeted += [place(x, y, zs[j], 1 - core) for j in range(4)]
-    greeted.append((mod(ta + 2 * core - 1, 16), ha, wa))
+    plane_xy.sort(key=lambda at: -hops[at[0]] - hops[at[1]])
+
+    def take(view, sem):
+        pltpu.make_async_copy(view, view, sem).wait()
+
+    greeted = []
     for dt in (-1, 1):
-        for row in (ha, other):
-            for dw in (-1, 0, 1):
-                if not (row is ha and dw == 0):
-                    greeted.append((mod(ta + dt, 16), row, mod(wa + dw, 4)))
+        for row in (other, ha):
+            for dw in (-1, 1, 0):
+                greeted.append((mod(ta + dt, 16), row, mod(wa + dw, 4)))
+    greeted += [place(x, y, zs[j], core) for j in (2, 1, 3)]
+    greeted += [(ta, other, mod(wa + dw, 4)) for dw in (-1, 1, 0)]
+    greeted += [(ta, ha, mod(wa + dw, 4)) for dw in (-1, 1)]
     for device in greeted:
         pl.semaphore_signal(barrier, inc=1, device_id=device, device_id_type=MESH)
 
@@ -104,7 +109,7 @@
 
     def halo_plain(n, src):
         copies = []
-        for slot, (dt, dh) in enumerate(((0, 1), (1, 0), (1, 1))):
+        for dt, dh in ((1, 1), (1, 0), (0, 1)):
             frames = pl.ds(edge_at[n], 2) if dt else pl.ds(0, T)
             to = pl.ds(halo_at[n], 2) if dt else pl.ds(own_at[n], T)
             rows = pl.ds(edge_row, 1) if dh else pl.ds(0, H)
@@ -113,7 +118,7 @@
                 remote(
                     src(frames, rows),
                     ext.at[n, to, to_rows, pl.ds(LEFT, W)],
-                    halo_send.at[n, slot], halo_recv.at[n, slot],
+                    halo_send.at[n, 0], halo_recv.at[n, 0],
                     (mod(ta + along[n] * dt, 16), other if dh else ha, wa),
                 )
             )
@@ -121,12 +126,9 @@
 
     def halo_columns(n):
         copies = []
-        slot = 3
-        for dt in (0, 1):
-            for dh in (0, 1):
+        for dt in (1, 0):
+            for dh in (1, 0):
                 for side, dw in ((0, -1), (1, 1)):
-                    if dt + dh + abs(dw) == 0:
-                        continue
                     frames = pl.ds(edge_at[n], 2) if dt else pl.ds(0, T)
                     to = pl.ds(halo_at[n], 2) if dt else pl.ds(own_at[n], T)
                     rows = pl.ds(edge_row, 1) if dh else pl.ds(0, H)
@@ -135,12 +137,17 @@
                         remote(
                             cols.at[n, side, frames, rows],
                             cols_ext.at[n, 1 - side, to, to_rows],
-                            halo_send.at[n, slot], halo_recv.at[n, slot],
+                            halo_send.at[n, 1], halo_recv.at[n, 1],
                             (mod(ta + along[n] * dt, 16), other if dh else ha, mod(wa + dw, 4)),
                         )
                     )
-                    slot += 1
         return copies
+
+    plain_rows = T * W + 2 * H * W + 2 * W
+
+    def halo_take(n, sems):
+        take(raw.at[0, pl.ds(0, plain_rows)], sems.at[n, 0])
+        take(cols_ext.at[n, :, :, pl.ds(0, H + 1)], sems.at[n, 1])
 
     def pack_columns(n):
         own = ext[n, pl.ds(own_at[n], T), pl.ds(1, H), pl.ds(LEFT, W)]
@@ -167,7 +174,7 @@
 
     pl.semaphore_wait(barrier, len(greeted))
     for n in (0, 1):
-        for copy in plain[n] + strips[n]:
+        for copy in strips[n] + plain[n]:
             copy.start()
 
     def transposed(value, ref):
@@ -280,7 +287,7 @@
 
     def line_start(f):
         copies = []
-        for step in (1, 2, 3):
+        for step in (2, 1, 3):
             for part, shard, device in (
                 (0, zs[step], place(x, y, zs[step], core)),
                 (1, ys[step], place(x, ys[step], z, core)),
@@ -288,16 +295,14 @@
                 copies.append(
                     remote(
                         summed.at[f, part, shard], line_recv.at[f, part, step - 1],
-                        line_send.at[f, part, step - 1], line_rcv.at[f, part, step - 1], device,
+                        line_send.at[f], line_rcv.at[f], device,
                     )
                 )
         for copy in copies:
             copy.start()
-        return copies
-
-    def line_end(f, copies):
-        for copy in copies:
-            copy.wait_recv()
+
+    def line_end(f):
+        take(line_recv.at[f], line_rcv.at[f])
         for part, own in ((0, z), (1, y)):
             line[f, part] = (summed[f, part, own] + line_recv[f, part, 0]) + (
                 line_recv[f, part, 1] + line_recv[f, part, 2]
@@ -311,56 +316,40 @@
 
     across = (y, z)
 
-    def plane_copies(f):
+    def plane_start(f):
         copies = []
         for part in (0, 1):
             mine = 4 * x + across[part]
-            for n, (i, j) in enumerate(plane_xy):
+            for i, j in plane_xy:
                 to = (ys, zs)[part][j]
                 device = place(xs[i], to, z, core) if part == 0 else place(xs[i], y, to, core)
                 copies.append(
                     remote(
                         line.at[f, part, rows8(piece(part, xs[i], to), 16)],
                         plane_recv.at[f, part, mine],
-                        plane_send.at[f, part, n], plane_rcv.at[f, part, mine], device,
+                        plane_send.at[f, part], plane_rcv.at[f, part], device,
                     )
                 )
-        return copies
-
-    def plane_start(f):
-        copies = plane_copies(f)
         for copy in copies:
             copy.start()
         for part in (0, 1):
             plane_recv[f, part, 4 * x + across[part]] = line[
                 f, part, rows8(piece(part, x, across[part]), 16)
             ]
-        return copies
 
     def plane_end(f):
         for part in (0, 1):
-            for n, (i, j) in enumerate(plane_xy):
-                source = (ys, zs)[part][j]
-                slot = 4 * xs[i] + source
-                device = (
-                    place(xs[i], source, z, core) if part == 0 else place(xs[i], y, source, core)
-                )
-                remote(
-                    line.at[f, part, pl.ds(0, 16)], plane_recv.at[f, part, slot],
-                    plane_send.at[f, part, n], plane_rcv.at[f, part, slot], device,
-                ).wait_recv()
+            take(plane_recv.at[f, part, pl.ds(0, 15)], plane_rcv.at[f, part])
             share[f, part] = jnp.sum(plane_recv[f, part], axis=0)
 
-    for copy in plain[0] + strips[0]:
-        copy.wait_recv()
+    halo_take(0, halo_recv)
     shift_columns(0)
     pre = conv(0, 0, False) + bias[...]
     pre_ref[...] = pre
     sig = 1.0 / (1.0 + jnp.exp(-pre))
     transposed(pre * sig, act_t)
 
-    for copy in plain[1] + strips[1]:
-        copy.wait_recv()
+    halo_take(1, halo_recv)
     shift_columns(1)
     weight_grad(act_t, 1, 0)
     swap0 = core_swap(0)
@@ -375,32 +364,40 @@
 
     swap0.wait_recv()
     core_add(0)
-    line0 = line_start(0)
+    line_start(0)
 
     plain.append(
         halo_plain(2, lambda t, h: ext.at[2, t, pl.ds(h.start + 1, h.size), pl.ds(LEFT, W)])
     )
     pack_columns(2)
     strips.append(halo_columns(2))
-    for copy in plain[2] + strips[2]:
+    for copy in strips[2] + plain[2]:
         copy.start()
 
     weight_grad(grad_t, 0, 1)
     swap1 = core_swap(1)
     swap1.wait_recv()
     core_add(1)
-    line1 = line_start(1)
-
-    line_end(0, line0)
-    plane0 = plane_start(0)
-
-    for copy in plain[2] + strips[2]:
-        copy.wait_recv()
+    line_start(1)
+
+    line_end(0)
+    plane_start(0)
+
+    halo_take(2, halo_recv)
     shift_columns(2)
     grad_input[...] = conv(2, 0, True).reshape(T, H, W, C)
 
-    line_end(1, line1)
-    plane1 = plane_start(1)
+    line_end(1)
+    plane_start(1)
+
+    for n in range(3):
+        halo_take(n, halo_send)
+    swap0.wait_send()
+    swap1.wait_send()
+    for f in range(2):
+        take(line_recv.at[f], line_send.at[f])
+    for part in range(2):
+        take(plane_recv.at[0, part, pl.ds(0, 15)], plane_send.at[0, part])
     plane_end(0)
     plane_end(1)
 
@@ -415,76 +412,68 @@
         )
         squares += keep_first * (share[f, 1, :8] * share[f, 1, :8])
         squares += keep_low * (share[f, 1, 8:] * share[f, 1, 8:])
-    note[:8] = squares
-    note[8:] = share[1, 1, 8:]
+    note[0:1] = jnp.sum(squares, axis=0, keepdims=True)
+    note[1:2] = jnp.sum(share[1, 1, 8:], axis=0, keepdims=True)
     here = 4 * x + y
     notes[here] = note[...]
 
-    def tell(n, i, j, slot):
-        return remote(
-            note, notes.at[slot], n_send.at[n], n_recv.at[slot], place(xs[i], ys[j], z, core)
-        )
-
-    for n, (i, j) in enumerate(plane_xy):
-        tell(n, i, j, here).start()
+    for i, j in plane_xy:
+        remote(
+            note, notes.at[here], n_send.at[0], n_recv.at[0], place(xs[i], ys[j], z, core)
+        ).start()
 
     wide = y // 2
     half_slot = 4 * lax.rem(y, 2) + x
 
     def give(i, j):
         return remote(
-            share, full.at[half_slot], ag_send.at[4 * i + j], ag_recv.at[half_slot],
+            share, full.at[half_slot], ag_send.at[0], ag_recv.at[0],
             place(2 * wide + i, ys[j], z, core),
         )
 
-    def each_give(act_on):
+    for j in (2, 1, 3, 0):
         for i in range(2):
-
-            @pl.when(2 * wide + i != x)
-            def _(i=i):
-                act_on(give(i, 0))
-
-            for j in (1, 2, 3):
-                act_on(give(i, j))
-
-    each_give(lambda copy: copy.start())
+            if j:
+                give(i, j).start()
+            else:
+
+                @pl.when(2 * wide + i != x)
+                def _(i=i):
+                    give(i, 0).start()
 
     @pl.when(wide == x_hi)
     def _():
         full[half_slot] = share[...]
 
-    for n, (i, j) in enumerate(plane_xy):
-        tell(n, i, j, 4 * xs[i] + ys[j]).wait_recv()
-    note2[:8] = jnp.sum(notes[:, :8], axis=0)
-    note2[8:] = notes[13, 8:]
+    take(notes.at[pl.ds(0, 15)], n_recv.at[0])
+    note2[0:1] = jnp.sum(notes[:, 0:1], axis=0)
+    note2[1:2] = notes[13, 1:2]
     there = 2 * z + core
     notes2[there] = note2[...]
-    line_zc = [(j, c) for j in range(4) for c in range(2) if j or c]
-
-    def tell2(n, j, c, slot):
-        to_core = 1 - core if c else core
-        return remote(
-            note2, notes2.at[slot], n2_send.at[n], n2_recv.at[slot], place(x, y, zs[j], to_core)
-        )
-
-    for n, (j, c) in enumerate(line_zc):
-        tell2(n, j, c, there).start()
-
+    for j, c in ((2, 1), (2, 0), (1, 1), (3, 1), (1, 0), (3, 0), (0, 1)):
+        remote(
+            note2, notes2.at[there], n_send.at[1], n_recv.at[1],
+            place(x, y, zs[j], 1 - core if c else core),
+        ).start()
+
+    def shares_take(sem):
+        @pl.when(wide == x_hi)
+        def _():
+            take(full.at[pl.ds(0, 7)], sem)
+
+        @pl.when(wide != x_hi)
+        def _():
+            take(full, sem)
+
+    shares_take(ag_recv.at[0])
+    shares_take(ag_send.at[0])
     for part in range(2):
-        for i in range(4):
-
-            @pl.when(jnp.logical_or(x != i, y != 2 * x_hi + part))
-            def _(part=part, i=i):
-                slot = 4 * part + i
-                remote(
-                    share, full.at[slot], ag_send.at[0], ag_recv.at[slot],
-                    place(x, ys[1], z, core),
-                ).wait_recv()
-
-    for n, (j, c) in enumerate(line_zc):
-        tell2(n, j, c, 2 * zs[j] + (1 - core if c else core)).wait_recv()
-    everything = jnp.sum(notes2[:, :8], axis=0)
-    raw_bias = jnp.sum(notes2[0, 8:], axis=0, keepdims=True)
+        take(plane_recv.at[1, part, pl.ds(0, 15)], plane_send.at[1, part])
+    take(notes.at[pl.ds(0, 15)], n_send.at[0])
+
+    take(notes2.at[pl.ds(0, 7)], n_recv.at[1])
+    everything = jnp.sum(notes2[:, 0:1], axis=0)
+    raw_bias = notes2[0, 1:2]
     norm2 = jnp.sum(everything, axis=(0, 1), keepdims=True) + jnp.sum(
         raw_bias * raw_bias, axis=(0, 1), keepdims=True
     )
@@ -498,14 +487,7 @@
             out[high : high + size] = full[slot, f, 1, :size] * factor
     grad_bias[...] = raw_bias * factor
 
-    for copies in plain + strips + [[swap0, swap1], line0, line1, plane0, plane1]:
-        for copy in copies:
-            copy.wait_send()
-    for n, (i, j) in enumerate(plane_xy):
-        tell(n, i, j, here).wait_send()
-    each_give(lambda copy: copy.wait_send())
-    for n, (j, c) in enumerate(line_zc):
-        tell2(n, j, c, there).wait_send()
+    take(notes2.at[pl.ds(0, 7)], n_send.at[1])
 
 
 def hand_over(*refs):
@@ -549,25 +531,23 @@
             vmem((2, 2, 16, 16, C), f32),
             vmem((2, 2, 16, C), f32),
             vmem((8, 2, 2, 16, C), f32),
-            vmem((16, C), f32),
-            vmem((16, 16, C), f32),
-            vmem((16, C), f32),
-            vmem((8, 16, C), f32),
+            vmem((2, C), f32),
+            vmem((16, 2, C), f32),
+            vmem((2, C), f32),
+            vmem((8, 2, C), f32),
             dma((4,)),
-            dma((3, 11)),
-            dma((3, 11)),
+            dma((3, 2)),
+            dma((3, 2)),
             dma((2,)),
             dma((2,)),
-            dma((2, 2, 3)),
-            dma((2, 2, 3)),
-            dma((2, 2, 15)),
-            dma((2, 2, 16)),
-            dma((8,)),
-            dma((8,)),
-            dma((15,)),
-            dma((16,)),
-            dma((7,)),
-            dma((8,)),
+            dma((2,)),
+            dma((2,)),
+            dma((2, 2)),
+            dma((2, 2)),
+            dma((1,)),
+            dma((1,)),
+            dma((2,)),
+            dma((2,)),
         ],
         compiler_params=pltpu.CompilerParams(
             collective_id=0, has_side_effects=True, vmem_limit_bytes=56 * 1024 * 1024

time: 63.5 us -> 57.6 us (0.907)
  Pallas kernels: 62.7 us -> 56.8 us
    pallas_call x1, Pallas kernels: 60.9 us -> 55 us  [per_device(): pl.pallas_call(kernel, out_shape=shapes, in_specs=[any_spec, any_spec, vm...]
where the time goes in v3:
time: 57.6 us; the launch traced here: 57.5 us
  Pallas kernels  56.8 us (99%)
  between operations  0.64 us (1%)
    pallas_call x1, Pallas kernels, per_device(): pl.pallas_call(kernel, out_shape=shapes, in_specs=[any_spec, any_spec, vm...  55 us
    pallas_call x1, Pallas kernels, per_device(): pl.pallas_call(hand_over, out_shape=shapes, in_specs=[vmem_spec] * 4, out...  1.81 us

profile of v3, /device:TPU:1, one launch (start us, length us, event | category | flops | bytes accessed | tf_op | source)
XLA Modules:
  0.0 57.5 jit_solution(14198177321092593253)
XLA Ops:
  0.6 55.0 %shard_map.84 = (f32[4,8,16,128]{3,2,1,0:T(8,128)}, f32[216,128]{1,0:T(8,128)}, f32[216,128]{1,0:T(8,128)}, f32[1,128]{1,0:T(1,128)}) custom-call(f32[4,8,16,128]{3,2,1,0:T(8,128)} %video.1, f32[27,128,128]{2,1,0:T(8,128)} %first.1, f32[1,128]{1,0:T(1,128)} %bitcast.2, f32[27,128,128]{2,1,0:T(8,128)} %second.1, f32[4,8,16,128]{3,2,1,0:T(8,128)} %cot.1), custom_call_target="tpu_custom_call" | custom-call | flops 2264924160 | bytes 6291456 | tf_op jit(solution)/shard_map/pallas_call | solution.py:509
  55.7 1.8 %shard_map.85 = (f32[4,8,16,128]{3,2,1,0:T(8,128)}, f32[216,128]{1,0:T(8,128)}, f32[216,128]{1,0:T(8,128)}, f32[1,128]{1,0:T(1,128)}) custom-call(f32[4,8,16,128]{3,2,1,0:T(8,128)} %get-tuple-element.12.refs_0_, f32[216,128]{1,0:T(8,128)} %get-tuple-element.13.refs_1_, f32[216,128]{1,0:T(8,128)} %get-tuple-element.14.refs_2_, f32[1,128]{1,0:T(1,128)} %get-tuple-element.15.refs_3_), custom_call_target="tpu_custom_call" | custom-call | tf_op jit(solution)/shard_map/pallas_call | solution.py:559

commit v4 on v3

--- a/solution.py
+++ b/solution.py
@@ -45,7 +45,7 @@
     grad_input, grad_first, grad_second, grad_bias,
     w_f32, w_split, ext, cols, cols_ext, shifted, acc, pre_ref, act_t, grad_t,
     raw, bias8, pack, summed, line_recv, line, plane_recv, share, full,
-    note, notes, note2, notes2,
+    note, notes, note2, notes2, bias_v, gi_v, g_v, gb_v,
     local_sem, halo_send, halo_recv, core_send, core_recv, line_send, line_rcv,
     plane_send, plane_rcv, ag_send, ag_recv, n_send, n_recv,
 ):
@@ -55,6 +55,33 @@
     z = ta // 4
     y = wa
     other = 1 - ha
+
+    barrier = pltpu.get_barrier_semaphore()
+    x = 2 * x_hi + ha
+
+    def place(px, py, pz, pc):
+        return (4 * pz + 2 * (px // 2) + pc, lax.rem(px, 2), py)
+
+    xs = [mod(x + step, 4) for step in range(4)]
+    ys = [mod(y + step, 4) for step in range(4)]
+    zs = [mod(z + step, 4) for step in range(4)]
+    hops = (0, 1, 2, 1)
+    plane_xy = [(i, j) for i in range(4) for j in range(4) if i or j]
+    plane_xy.sort(key=lambda at: -hops[at[0]] - hops[at[1]])
+
+    def take(view, sem):
+        pltpu.make_async_copy(view, view, sem).wait()
+
+    greeted = []
+    for dt in (-1, 1):
+        for row in (other, ha):
+            for dw in (-1, 1, 0):
+                greeted.append((mod(ta + dt, 16), row, mod(wa + dw, 4)))
+    greeted += [place(x, y, zs[j], core) for j in (2, 1, 3)]
+    greeted += [(ta, other, mod(wa + dw, 4)) for dw in (-1, 1, 0)]
+    greeted += [(ta, ha, mod(wa + dw, 4)) for dw in (-1, 1)]
+    for device in greeted:
+        pl.semaphore_signal(barrier, inc=1, device_id=device, device_id_type=MESH)
 
     own_at = (2, 0, 0)
     blocks = [
@@ -67,40 +94,14 @@
         pltpu.make_async_copy(src, w_f32.at[n], local_sem.at[2 + n])
         for n, src in enumerate((first, second))
     ]
-    for copy in blocks + loads:
+    bias_load = pltpu.make_async_copy(bias, bias_v, local_sem.at[4])
+    for copy in blocks + [bias_load] + loads:
         copy.start()
 
     gap = 9 * ha
     for n in range(3):
         ext[n, :, pl.ds(gap, 1)] = jnp.zeros((T + 2, 1, 32, C), f32)
         cols_ext[n, :, :, pl.ds(gap, 1)] = jnp.zeros((2, T + 2, 1, 1, C), f32)
-
-    barrier = pltpu.get_barrier_semaphore()
-    x = 2 * x_hi + ha
-
-    def place(px, py, pz, pc):
-        return (4 * pz + 2 * (px // 2) + pc, lax.rem(px, 2), py)
-
-    xs = [mod(x + step, 4) for step in range(4)]
-    ys = [mod(y + step, 4) for step in range(4)]
-    zs = [mod(z + step, 4) for step in range(4)]
-    hops = (0, 1, 2, 1)
-    plane_xy = [(i, j) for i in range(4) for j in range(4) if i or j]
-    plane_xy.sort(key=lambda at: -hops[at[0]] - hops[at[1]])
-
-    def take(view, sem):
-        pltpu.make_async_copy(view, view, sem).wait()
-
-    greeted = []
-    for dt in (-1, 1):
-        for row in (other, ha):
-            for dw in (-1, 1, 0):
-                greeted.append((mod(ta + dt, 16), row, mod(wa + dw, 4)))
-    greeted += [place(x, y, zs[j], core) for j in (2, 1, 3)]
-    greeted += [(ta, other, mod(wa + dw, 4)) for dw in (-1, 1, 0)]
-    greeted += [(ta, ha, mod(wa + dw, 4)) for dw in (-1, 1)]
-    for device in greeted:
-        pl.semaphore_signal(barrier, inc=1, device_id=device, device_id_type=MESH)
 
     halo_at = (0, 4, 4)
     edge_at = (2, 0, 0)
@@ -162,6 +163,7 @@
 
     for copy in loads:
         copy.wait()
+    bias_load.wait()
 
     def split_filters(tap, _):
         for n in range(2):
@@ -239,17 +241,17 @@
         return acc[:, :C] + acc[:, C:]
 
     def weight_grad(fixed, n, f):
-        def taps(step, _):
-            p, q = step // 3, lax.rem(step, 3)
-            for c in range(3):
+        def taps(p, _):
+            for m in range(9):
+                q, c = m // 3, m % 3
                 at = (p, q, c) if f else (2 - p, 2 - q, 2 - c)
                 window = shifted[n, at[2], pl.ds(at[0], T), pl.ds(at[1], H)].reshape(V, 2 * C)
                 o = jnp.dot(fixed[...], window, preferred_element_type=f32)
                 o = (o[:C, :C] + o[C:, :C]) + (o[:C, C:] + o[C:, C:])
-                raw[f, rows8((3 * step + c) * C, C)] = o.T if f else o
+                raw[f, rows8((9 * p + m) * C, C)] = o.T if f else o
             return 0
 
-        lax.fori_loop(0, 9, taps, 0)
+        lax.fori_loop(0, 3, taps, 0)
 
     pieces = ((0, HALF), (HALF, QUART), (HALF + QUART, QUART - 8))
 
@@ -317,12 +319,13 @@
     across = (y, z)
 
     def plane_start(f):
-        copies = []
+        copies, far = [], []
         for part in (0, 1):
             mine = 4 * x + across[part]
             for i, j in plane_xy:
                 to = (ys, zs)[part][j]
                 device = place(xs[i], to, z, core) if part == 0 else place(xs[i], y, to, core)
+                far.append(-hops[i] - hops[j])
                 copies.append(
                     remote(
                         line.at[f, part, rows8(piece(part, xs[i], to), 16)],
@@ -330,8 +333,8 @@
                         plane_send.at[f, part], plane_rcv.at[f, part], device,
                     )
                 )
-        for copy in copies:
-            copy.start()
+        for n in sorted(range(30), key=lambda n: far[n]):
+            copies[n].start()
         for part in (0, 1):
             plane_recv[f, part, 4 * x + across[part]] = line[
                 f, part, rows8(piece(part, x, across[part]), 16)
@@ -344,7 +347,7 @@
 
     halo_take(0, halo_recv)
     shift_columns(0)
-    pre = conv(0, 0, False) + bias[...]
+    pre = conv(0, 0, False) + bias_v[...]
     pre_ref[...] = pre
     sig = 1.0 / (1.0 + jnp.exp(-pre))
     transposed(pre * sig, act_t)
@@ -366,6 +369,12 @@
     core_add(0)
     line_start(0)
 
+    weight_grad(grad_t, 0, 1)
+    swap1 = core_swap(1)
+    swap1.wait_recv()
+    core_add(1)
+    line_start(1)
+
     plain.append(
         halo_plain(2, lambda t, h: ext.at[2, t, pl.ds(h.start + 1, h.size), pl.ds(LEFT, W)])
     )
@@ -374,18 +383,14 @@
     for copy in strips[2] + plain[2]:
         copy.start()
 
-    weight_grad(grad_t, 0, 1)
-    swap1 = core_swap(1)
-    swap1.wait_recv()
-    core_add(1)
-    line_start(1)
-
     line_end(0)
     plane_start(0)
 
-    halo_take(2, halo_recv)
-    shift_columns(2)
-    grad_input[...] = conv(2, 0, True).reshape(T, H, W, C)
+    def input_grad():
+        gi_v[...] = conv(2, 0, True).reshape(T, H, W, C)
+        gi_out.start()
+
+    gi_out = pltpu.make_async_copy(gi_v, grad_input, local_sem.at[5])
 
     line_end(1)
     plane_start(1)
@@ -399,6 +404,9 @@
     for part in range(2):
         take(plane_recv.at[0, part, pl.ds(0, 15)], plane_send.at[0, part])
     plane_end(0)
+    halo_take(2, halo_recv)
+    shift_columns(2)
+    input_grad()
     plane_end(1)
 
     last = x == 3
@@ -478,14 +486,25 @@
         raw_bias * raw_bias, axis=(0, 1), keepdims=True
     )
     factor = jnp.minimum(1.0, jnp.sqrt(jnp.full((1, 1), LIMIT, f32)) / jnp.sqrt(norm2))
-    for f, out in ((0, grad_second), (1, grad_first)):
+    for f in range(2):
+        out = g_v.at[f]
         for slot in range(8):
             low = 16 * min(slot, 6)
             out[low : low + 16] = full[slot, f, 0] * factor
             high = HALF + QUART * (slot // 4) + min(16 * (slot % 4), 40)
             size = min(16, OWN - high)
             out[high : high + size] = full[slot, f, 1, :size] * factor
-    grad_bias[...] = raw_bias * factor
+    gb_v[...] = raw_bias * factor
+    lasts = [
+        pltpu.make_async_copy(src, dst, local_sem.at[n])
+        for n, (src, dst) in enumerate(
+            ((g_v.at[1], grad_first), (g_v.at[0], grad_second), (gb_v, grad_bias))
+        )
+    ]
+    for copy in lasts:
+        copy.start()
+    for copy in lasts + [gi_out]:
+        copy.wait()
 
     take(notes2.at[pl.ds(0, 7)], n_send.at[1])
 
@@ -509,8 +528,8 @@
     outs = pl.pallas_call(
         kernel,
         out_shape=shapes,
-        in_specs=[any_spec, any_spec, vmem_spec, any_spec, any_spec],
-        out_specs=[vmem_spec] * 4,
+        in_specs=[any_spec] * 5,
+        out_specs=[any_spec] * 4,
         scratch_shapes=[
             vmem((2, 27, C, C), f32),
             vmem((2, 27, C, 2 * C), bf16),
@@ -535,7 +554,11 @@
             vmem((16, 2, C), f32),
             vmem((2, C), f32),
             vmem((8, 2, C), f32),
-            dma((4,)),
+            vmem((1, C), f32),
+            vmem((T, H, W, C), f32),
+            vmem((2, OWN, C), f32),
+            vmem((1, C), f32),
+            dma((6,)),
             dma((3, 2)),
             dma((3, 2)),
             dma((2,)),

time: 57.6 us -> 54.4 us (0.944)
  Pallas kernels: 56.8 us -> 53.6 us
    pallas_call x1, Pallas kernels: 55 us -> 51.8 us  [per_device(): pl.pallas_call(kernel, out_shape=shapes, in_specs=[any_spec] * 5, out_spe...]
where the time goes in v4:
time: 54.4 us; the launch traced here: 54.2 us
  Pallas kernels  53.6 us (99%)
  between operations  0.64 us (1%)
    pallas_call x1, Pallas kernels, per_device(): pl.pallas_call(kernel, out_shape=shapes, in_specs=[any_spec] * 5, out_spe...  51.8 us
    pallas_call x1, Pallas kernels, per_device(): pl.pallas_call(hand_over, out_shape=shapes, in_specs=[vmem_spec] * 4, out...  1.81 us

profile of v4, /device:TPU:1, one launch (start us, length us, event | category | flops | bytes accessed | tf_op | source)
XLA Modules:
  0.0 54.2 jit_solution(5131106841565570111)
XLA Ops:
  0.6 51.8 %shard_map.84 = (f32[4,8,16,128]{3,2,1,0:T(8,128)}, f32[216,128]{1,0:T(8,128)}, f32[216,128]{1,0:T(8,128)}, f32[1,128]{1,0:T(1,128)}) custom-call(f32[4,8,16,128]{3,2,1,0:T(8,128)} %video.1, f32[27,128,128]{2,1,0:T(8,128)} %first.1, f32[1,128]{1,0:T(1,128)} %bitcast.2, f32[27,128,128]{2,1,0:T(8,128)} %second.1, f32[4,8,16,128]{3,2,1,0:T(8,128)} %cot.1), custom_call_target="tpu_custom_call" | custom-call | flops 2264924160 | bytes 6291456 | tf_op jit(solution)/shard_map/pallas_call | solution.py:528
  52.4 1.8 %shard_map.85 = (f32[4,8,16,128]{3,2,1,0:T(8,128)}, f32[216,128]{1,0:T(8,128)}, f32[216,128]{1,0:T(8,128)}, f32[1,128]{1,0:T(1,128)}) custom-call(f32[4,8,16,128]{3,2,1,0:T(8,128)} %get-tuple-element.12.refs_0_, f32[216,128]{1,0:T(8,128)} %get-tuple-element.13.refs_1_, f32[216,128]{1,0:T(8,128)} %get-tuple-element.14.refs_2_, f32[1,128]{1,0:T(1,128)} %get-tuple-element.15.refs_3_), custom_call_target="tpu_custom_call" | custom-call | tf_op jit(solution)/shard_map/pallas_call | solution.py:582

commit v5 on v4

--- a/solution.py
+++ b/solution.py
@@ -13,8 +13,8 @@
 ROWS = 27 * C
 OWN = ROWS // 16
 PAD = OWN + 8
-HALF = PAD // 2
-QUART = HALF // 2
+FIRST, SECOND, THIRD = 80, 40, 32
+SHARD = (2 * FIRST, 4 * SECOND, 4 * THIRD)
 LEFT = 8
 LIMIT = float(54 * C * C + C)
 
@@ -44,7 +44,7 @@
     video, first, bias, second, cot,
     grad_input, grad_first, grad_second, grad_bias,
     w_f32, w_split, ext, cols, cols_ext, shifted, acc, pre_ref, act_t, grad_t,
-    raw, bias8, pack, summed, line_recv, line, plane_recv, share, full,
+    raw, bias8, pack, summed, line_recv, line, plane_recv, share, full, third,
     note, notes, note2, notes2, bias_v, gi_v, g_v, gb_v,
     local_sem, halo_send, halo_recv, core_send, core_recv, line_send, line_rcv,
     plane_send, plane_rcv, ag_send, ag_recv, n_send, n_recv,
@@ -253,13 +253,21 @@
 
         lax.fori_loop(0, 3, taps, 0)
 
-    pieces = ((0, HALF), (HALF, QUART), (HALF + QUART, QUART - 8))
+    pieces = (
+        (0, FIRST),
+        (FIRST, SECOND),
+        (FIRST + SECOND, SECOND),
+        (FIRST + 2 * SECOND, THIRD),
+        (FIRST + 2 * SECOND + THIRD, THIRD - 8),
+    )
 
     def slots(kz, kx):
         return (
-            (0, kz, kx * HALF),
-            (1, 2 * kx, kz * QUART),
-            (1, 2 * kx + 1, kz * QUART),
+            (0, kz, kx * FIRST),
+            (1, 2 * kx, kz * SECOND),
+            (1, 2 * kx + 1, kz * SECOND),
+            (2, 2 * kx, kz * THIRD),
+            (2, 2 * kx + 1, kz * THIRD),
         )
 
     owners = [(kz, kx) for kz in range(4) for kx in range(2)]
@@ -269,8 +277,8 @@
             k = 4 * kz + 2 * kx + 1 - core
             for (start, size), (part, shard, to) in zip(pieces, slots(kz, kx)):
                 pack[f, part, shard, to : to + size] = raw[f, rows8(OWN * k + start, size)]
-            tail = kz * QUART + QUART - 8
-            pack[f, 1, 2 * kx + 1, tail : tail + 8] = bias8[...] if f else jnp.zeros((8, C), f32)
+            tail = (kz + 1) * THIRD - 8
+            pack[f, 2, 2 * kx + 1, tail : tail + 8] = bias8[...] if f else jnp.zeros((8, C), f32)
         copy = remote(
             pack.at[f], summed.at[f], core_send.at[f], core_recv.at[f],
             (ta + 1 - 2 * core, ha, wa),
@@ -284,66 +292,77 @@
             for (start, size), (part, shard, to) in zip(pieces, slots(kz, kx)):
                 summed[f, part, shard, to : to + size] += raw[f, rows8(OWN * k + start, size)]
             if f:
-                tail = kz * QUART + QUART - 8
-                summed[f, 1, 2 * kx + 1, tail : tail + 8] += bias8[...]
+                tail = (kz + 1) * THIRD - 8
+                summed[f, 2, 2 * kx + 1, tail : tail + 8] += bias8[...]
 
     def line_start(f):
-        copies = []
         for step in (2, 1, 3):
             for part, shard, device in (
                 (0, zs[step], place(x, y, zs[step], core)),
                 (1, ys[step], place(x, ys[step], z, core)),
+                (2, xs[step], place(xs[step], y, z, core)),
             ):
-                copies.append(
-                    remote(
-                        summed.at[f, part, shard], line_recv.at[f, part, step - 1],
-                        line_send.at[f], line_rcv.at[f], device,
-                    )
+                size = pl.ds(0, SHARD[part])
+                remote(
+                    summed.at[f, part, shard, size], line_recv.at[f, part, step - 1, size],
+                    line_send.at[f, part], line_rcv.at[f, part], device,
+                ).start()
+
+    def line_take(f, sems):
+        for part in range(3):
+            take(line_recv.at[f, part, :, pl.ds(0, SHARD[part])], sems.at[f, part])
+
+    def line_end(f):
+        line_take(f, line_rcv)
+        for part, own in ((0, z), (1, y), (2, x)):
+            size = SHARD[part]
+            line[f, part, :size] = (
+                summed[f, part, own, :size] + line_recv[f, part, 0, :size]
+            ) + (line_recv[f, part, 1, :size] + line_recv[f, part, 2, :size])
+
+    def piece(part, one, two):
+        if part == 0:
+            return (two // 2) * FIRST + 16 * jnp.minimum(4 * lax.rem(two, 2) + one, 4)
+        if part == 1:
+            return two * SECOND + jnp.minimum(16 * one, SECOND - 16)
+        return two * THIRD + jnp.minimum(16 * one, THIRD - 16)
+
+    sides = ((xs, ys), (xs, zs), (ys, zs))
+
+    def plane_start(f):
+        copies = []
+        for part in range(3):
+            ones, twos = sides[part]
+            mine = 4 * ones[0] + twos[0]
+            for i, j in plane_xy:
+                one, two = ones[i], twos[j]
+                device = (
+                    place(one, two, z, core),
+                    place(one, y, two, core),
+                    place(x, one, two, core),
+                )[part]
+                copy = remote(
+                    line.at[f, part, rows8(piece(part, one, two), 16)],
+                    plane_recv.at[f, part, mine],
+                    plane_send.at[f, part], plane_rcv.at[f, part], device,
                 )
-        for copy in copies:
+                copies.append((-hops[i] - hops[j], len(copies), copy))
+        for _, _, copy in sorted(copies, key=lambda entry: entry[:2]):
             copy.start()
-
-    def line_end(f):
-        take(line_recv.at[f], line_rcv.at[f])
-        for part, own in ((0, z), (1, y)):
-            line[f, part] = (summed[f, part, own] + line_recv[f, part, 0]) + (
-                line_recv[f, part, 1] + line_recv[f, part, 2]
-            )
-
-    def piece(part, px, other_axis):
-        if part == 0:
-            slot = 4 * lax.rem(other_axis, 2) + px
-            return (other_axis // 2) * HALF + 16 * jnp.minimum(slot, 6)
-        return other_axis * QUART + jnp.minimum(16 * px, 40)
-
-    across = (y, z)
-
-    def plane_start(f):
-        copies, far = [], []
-        for part in (0, 1):
-            mine = 4 * x + across[part]
-            for i, j in plane_xy:
-                to = (ys, zs)[part][j]
-                device = place(xs[i], to, z, core) if part == 0 else place(xs[i], y, to, core)
-                far.append(-hops[i] - hops[j])
-                copies.append(
-                    remote(
-                        line.at[f, part, rows8(piece(part, xs[i], to), 16)],
-                        plane_recv.at[f, part, mine],
-                        plane_send.at[f, part], plane_rcv.at[f, part], device,
-                    )
-                )
-        for n in sorted(range(30), key=lambda n: far[n]):
-            copies[n].start()
-        for part in (0, 1):
-            plane_recv[f, part, 4 * x + across[part]] = line[
-                f, part, rows8(piece(part, x, across[part]), 16)
+        for part in range(3):
+            ones, twos = sides[part]
+            plane_recv[f, part, 4 * ones[0] + twos[0]] = line[
+                f, part, rows8(piece(part, ones[0], twos[0]), 16)
             ]
 
+    def plane_take(f, sems):
+        for part in range(3):
+            take(plane_recv.at[f, part, pl.ds(0, 15)], sems.at[f, part])
+
     def plane_end(f):
-        for part in (0, 1):
-            take(plane_recv.at[f, part, pl.ds(0, 15)], plane_rcv.at[f, part])
-            share[f, part] = jnp.sum(plane_recv[f, part], axis=0)
+        plane_take(f, plane_rcv)
+        for part in range(3):
+            share[part, f] = jnp.sum(plane_recv[f, part], axis=0)
 
     halo_take(0, halo_recv)
     shift_columns(0)
@@ -369,20 +388,23 @@
     core_add(0)
     line_start(0)
 
+    def send_halo():
+        plain.append(
+            halo_plain(2, lambda t, h: ext.at[2, t, pl.ds(h.start + 1, h.size), pl.ds(LEFT, W)])
+        )
+        pack_columns(2)
+        strips.append(halo_columns(2))
+        for copy in strips[2] + plain[2]:
+            copy.start()
+
+
     weight_grad(grad_t, 0, 1)
     swap1 = core_swap(1)
     swap1.wait_recv()
     core_add(1)
     line_start(1)
 
-    plain.append(
-        halo_plain(2, lambda t, h: ext.at[2, t, pl.ds(h.start + 1, h.size), pl.ds(LEFT, W)])
-    )
-    pack_columns(2)
-    strips.append(halo_columns(2))
-    for copy in strips[2] + plain[2]:
-        copy.start()
-
+    send_halo()
     line_end(0)
     plane_start(0)
 
@@ -395,33 +417,30 @@
     line_end(1)
     plane_start(1)
 
-    for n in range(3):
+    for n in range(2):
         halo_take(n, halo_send)
     swap0.wait_send()
     swap1.wait_send()
     for f in range(2):
-        take(line_recv.at[f], line_send.at[f])
-    for part in range(2):
-        take(plane_recv.at[0, part, pl.ds(0, 15)], plane_send.at[0, part])
+        line_take(f, line_send)
+    plane_take(0, plane_send)
     plane_end(0)
     halo_take(2, halo_recv)
     shift_columns(2)
-    input_grad()
     plane_end(1)
 
-    last = x == 3
-    odd = lax.rem(y, 2) == 1
-    keep_low = jnp.where(jnp.logical_and(last, odd), 0.0, 1.0)
-    keep_first = jnp.where(last, 0.0, 1.0)
+    keeps = (
+        (4 * lax.rem(y, 2) + x < 5,) * 2,
+        (x < 2, x < 3),
+        (y < 2, y + ha < 2),
+    )
     squares = jnp.zeros((8, C), f32)
-    for f in range(2):
-        squares += keep_low * (
-            share[f, 0, :8] * share[f, 0, :8] + share[f, 0, 8:] * share[f, 0, 8:]
-        )
-        squares += keep_first * (share[f, 1, :8] * share[f, 1, :8])
-        squares += keep_low * (share[f, 1, 8:] * share[f, 1, 8:])
+    for part in range(3):
+        for half in range(2):
+            mine = share[part, :, 8 * half : 8 * half + 8]
+            squares += jnp.where(keeps[part][half], 1.0, 0.0) * jnp.sum(mine * mine, axis=0)
     note[0:1] = jnp.sum(squares, axis=0, keepdims=True)
-    note[1:2] = jnp.sum(share[1, 1, 8:], axis=0, keepdims=True)
+    note[1:2] = jnp.sum(share[2, 1, 8:], axis=0, keepdims=True)
     here = 4 * x + y
     notes[here] = note[...]
 
@@ -435,7 +454,7 @@
 
     def give(i, j):
         return remote(
-            share, full.at[half_slot], ag_send.at[0], ag_recv.at[0],
+            share.at[pl.ds(0, 2)], full.at[half_slot], ag_send.at[0], ag_recv.at[0],
             place(2 * wide + i, ys[j], z, core),
         )
 
@@ -449,13 +468,24 @@
                 def _(i=i):
                     give(i, 0).start()
 
+    third_slot = 4 * ha + y
+    for j in (2, 1, 3, 0):
+        for row in (other, ha):
+            if j or row is other:
+                remote(
+                    share.at[2], third.at[third_slot], ag_send.at[1], ag_recv.at[1],
+                    (ta, row, ys[j]),
+                ).start()
+    third[third_slot] = share[2]
+
     @pl.when(wide == x_hi)
     def _():
-        full[half_slot] = share[...]
-
+        full[half_slot] = share[:2]
+
+    input_grad()
     take(notes.at[pl.ds(0, 15)], n_recv.at[0])
     note2[0:1] = jnp.sum(notes[:, 0:1], axis=0)
-    note2[1:2] = notes[13, 1:2]
+    note2[1:2] = notes[5, 1:2]
     there = 2 * z + core
     notes2[there] = note2[...]
     for j, c in ((2, 1), (2, 0), (1, 1), (3, 1), (1, 0), (3, 0), (0, 1)):
@@ -464,7 +494,10 @@
             place(x, y, zs[j], 1 - core if c else core),
         ).start()
 
-    def shares_take(sem):
+    def shares_take(sems):
+        sem = sems.at[0]
+        take(third.at[pl.ds(0, 7)], sems.at[1])
+
         @pl.when(wide == x_hi)
         def _():
             take(full.at[pl.ds(0, 7)], sem)
@@ -473,10 +506,9 @@
         def _():
             take(full, sem)
 
-    shares_take(ag_recv.at[0])
-    shares_take(ag_send.at[0])
-    for part in range(2):
-        take(plane_recv.at[1, part, pl.ds(0, 15)], plane_send.at[1, part])
+    shares_take(ag_recv)
+    shares_take(ag_send)
+    plane_take(1, plane_send)
     take(notes.at[pl.ds(0, 15)], n_send.at[0])
 
     take(notes2.at[pl.ds(0, 7)], n_recv.at[1])
@@ -489,11 +521,14 @@
     for f in range(2):
         out = g_v.at[f]
         for slot in range(8):
-            low = 16 * min(slot, 6)
-            out[low : low + 16] = full[slot, f, 0] * factor
-            high = HALF + QUART * (slot // 4) + min(16 * (slot % 4), 40)
-            size = min(16, OWN - high)
-            out[high : high + size] = full[slot, f, 1, :size] * factor
+            half, at = slot // 4, 16 * (slot % 4)
+            low = 16 * min(slot, 4)
+            out[low : low + 16] = full[slot, 0, f] * factor
+            low = FIRST + SECOND * half + min(at, SECOND - 16)
+            out[low : low + 16] = full[slot, 1, f] * factor
+            low = FIRST + 2 * SECOND + THIRD * half + min(at, THIRD - 16)
+            size = min(16, OWN - low)
+            out[low : low + size] = third[slot, f, :size] * factor
     gb_v[...] = raw_bias * factor
     lasts = [
         pltpu.make_async_copy(src, dst, local_sem.at[n])
@@ -507,6 +542,7 @@
         copy.wait()
 
     take(notes2.at[pl.ds(0, 7)], n_send.at[1])
+    halo_take(2, halo_send)
 
 
 def hand_over(*refs):
@@ -543,13 +579,14 @@
             vmem((2 * C, V), bf16),
             vmem((2, ROWS, C), f32),
             vmem((8, C), f32),
-            vmem((2, 2, 4, PAD, C), f32),
-            vmem((2, 2, 4, PAD, C), f32),
-            vmem((2, 2, 3, PAD, C), f32),
-            vmem((2, 2, PAD, C), f32),
-            vmem((2, 2, 16, 16, C), f32),
-            vmem((2, 2, 16, C), f32),
+            vmem((2, 3, 4, SHARD[0], C), f32),
+            vmem((2, 3, 4, SHARD[0], C), f32),
+            vmem((2, 3, 3, SHARD[0], C), f32),
+            vmem((2, 3, SHARD[0], C), f32),
+            vmem((2, 3, 16, 16, C), f32),
+            vmem((3, 2, 16, C), f32),
             vmem((8, 2, 2, 16, C), f32),
+            vmem((8, 2, 16, C), f32),
             vmem((2, C), f32),
             vmem((16, 2, C), f32),
             vmem((2, C), f32),
@@ -563,12 +600,12 @@
             dma((3, 2)),
             dma((2,)),
             dma((2,)),
+            dma((2, 3)),
+            dma((2, 3)),
+            dma((2, 3)),
+            dma((2, 3)),
             dma((2,)),
             dma((2,)),
-            dma((2, 2)),
-            dma((2, 2)),
-            dma((1,)),
-            dma((1,)),
             dma((2,)),
             dma((2,)),
         ],

time: 54.4 us -> 54.2 us (level)
  no operation moved by 1% of the time
where the time goes in v5:
time: 54.2 us; the launch traced here: 54.1 us
  Pallas kernels  53.4 us (99%)
  between operations  0.64 us (1%)
    pallas_call x1, Pallas kernels, per_device(): pl.pallas_call(kernel, out_shape=shapes, in_specs=[any_spec] * 5, out_spe...  51.6 us
    pallas_call x1, Pallas kernels, per_device(): pl.pallas_call(hand_over, out_shape=shapes, in_specs=[vmem_spec] * 4, out...  1.81 us

profile of v5, /device:TPU:1, one launch (start us, length us, event | category | flops | bytes accessed | tf_op | source)
XLA Modules:
  0.0 54.1 jit_solution(15225732279291611992)
XLA Ops:
  0.6 51.6 %shard_map.84 = (f32[4,8,16,128]{3,2,1,0:T(8,128)}, f32[216,128]{1,0:T(8,128)}, f32[216,128]{1,0:T(8,128)}, f32[1,128]{1,0:T(1,128)}) custom-call(f32[4,8,16,128]{3,2,1,0:T(8,128)} %video.1, f32[27,128,128]{2,1,0:T(8,128)} %first.1, f32[1,128]{1,0:T(1,128)} %bitcast.2, f32[27,128,128]{2,1,0:T(8,128)} %second.1, f32[4,8,16,128]{3,2,1,0:T(8,128)} %cot.1), custom_call_target="tpu_custom_call" | custom-call | flops 2264924160 | bytes 6291456 | tf_op jit(solution)/shard_map/pallas_call | solution.py:564
  52.3 1.8 %shard_map.85 = (f32[4,8,16,128]{3,2,1,0:T(8,128)}, f32[216,128]{1,0:T(8,128)}, f32[216,128]{1,0:T(8,128)}, f32[1,128]{1,0:T(1,128)}) custom-call(f32[4,8,16,128]{3,2,1,0:T(8,128)} %get-tuple-element.12.refs_0_, f32[216,128]{1,0:T(8,128)} %get-tuple-element.13.refs_1_, f32[216,128]{1,0:T(8,128)} %get-tuple-element.14.refs_2_, f32[1,128]{1,0:T(1,128)} %get-tuple-element.15.refs_3_), custom_call_target="tpu_custom_call" | custom-call | tf_op jit(solution)/shard_map/pallas_call | solution.py:619
